TPU v7x, 512 devices: a whole 4x4x16 slice. The times are simulated.
512 devices in a mesh: rows: 32 (over x, y, core), bands: 16 (over z).
Axes of the slice: x: 4, y: 4, z: 16, core: 2. Of those that a mesh axis runs over, the one named last changes fastest.
Arguments:
- psi_panels: float32 [32768, 256], P('rows', 'bands'), may hold values from -6 to 6
- rotation: float32 [256, 8000], P('rows', 'bands'), may hold values from -0.375 to 0.375
- accumulated: float32 [32768, 8000], P('rows', 'bands'), may hold values from -6 to 6
Outputs:
- rotated: float32 [32768, 8000], P('rows', 'bands')
All inputs are finite; a program needn't handle non-finite values.
Results may differ from a plain program's by a relative error of at most 0.000059.
Values sent between devices are 32-bit elements; how exact they have to be, the bound alone decides.
No kernel may reach another device: no remote copies, remote signals or barrier semaphores. Data moves between devices by JAX's collectives and lax.ppermute only.
A program may use at most 64 MiB of HBM per device.

v0:
```python
import jax
import jax.numpy as jnp
from jax import lax
from jax.sharding import PartitionSpec as P


def multiply(left, right):
    return jnp.dot(left, right, precision=lax.Precision.HIGHEST, preferred_element_type=jnp.float32)


def local(psi_panels, rotation, accumulated):
    psi_whole = lax.all_gather(psi_panels, "bands", axis=1, tiled=True)
    rot_whole = lax.all_gather(rotation, "rows", axis=0, tiled=True)
    rotated = accumulated + multiply(psi_whole, rot_whole)
    return rotated


def solution(mesh):
    in_specs = (P("rows", "bands"), P("rows", "bands"), P("rows", "bands"))
    out_specs = P("rows", "bands")
    return jax.shard_map(local, mesh=mesh, in_specs=in_specs, out_specs=out_specs, check_vma=False)
```

profile of v0, /device:TPU:4, one launch (start us, length us, event | category | flops | bytes accessed | tf_op | source)
XLA Modules:
  0.0 96.9 jit_solution(10149607497188163887)
XLA Ops:
  6.5 0.0 all-gather.2.cloned.1.call-start
  6.5 0.7 all-gather.2.cloned.1.call-update
  7.3 26.3 %all_gather.7 = f32[256,500]{1,0:T(8,128)S(1)} all-gather(f32[8,500]{1,0:T(8,128)} %param.4), channel_id=1, replica_groups=mesh['rows'=32,'bands'=16] {'rows'}, dimensions={0}, use_global_device_ids=true | all-gather | bytes 528000 | tf_op jit(solution)/shard_map/all_gather | solution.py:13
  33.5 51.4 %all-gather.2.cloned.1.call-done = f32[1024,256]{0,1:T(8,128)} async-done(((f32[1024,16]{0,1:T(8,128)}), f32[1024,256]{0,1:T(8,128)}) %all-gather.2.cloned.1.call-update) | async-done | bytes 1048592 | tf_op jit(solution)/shard_map/all_gather | solution.py:12
  84.9 5.1 %convolution_add_fusion = f32[1024,500]{0,1:T(8,128)} fusion(f32[1024,500]{0,1:T(8,128)} %param.5, f32[1024,256]{0,1:T(8,128)} %all-gather.2.cloned.1.call-done, f32[256,500]{1,0:T(8,128)S(1)} %all_gather.7), kind=kOutput, calls=%fused_computation | convolution fusion | flops 1573376000 | bytes 5656576 | tf_op jit(solution)/shard_map/dot_general | solution.py:8
Async XLA Ops:
  6.5 78.4 %all-gather.2.cloned.1.call-start = ((), (), s32[]{:S(2)}) async-start(), calls=%async_computation | async-start | bytes 1114112 | tf_op jit(solution)/shard_map/all_gather | solution.py:12
Sparse Core Ops, SparseCore 0:
  9.4 75.4 all-gather.1
where the time goes:
time: 97.1 us; the launch traced here: 96.9 us
  waiting for transfers between devices  52.1 us (54%)
  blocking collectives  26.3 us (27%)
  between operations  13.4 us (14%)
  matrix products  5.06 us (5%)
    all_gather x1, waiting for transfers between devices, local(): psi_whole = lax.all_gather(psi_panels, 'bands', axis=1, tiled=True)  51.4 us
    all_gather x1, blocking collectives, local(): rot_whole = lax.all_gather(rotation, 'rows', axis=0, tiled=True)  26.3 us
    dot_general x1, matrix products, multiply(): jnp.dot(left, right, precision=lax.Precision.HIGHEST, preferred_element_t...  5.06 us
  transfers between devices with their start and end apart: 1, of which 1 were waited for; matrix products, arithmetic and copies ran while one was open for 0% of the time, Pallas kernels for 0%

commit v1 on v0

v1 whole, which is shorter than its diff:
```python
import jax
import jax.numpy as jnp
from jax import lax
from jax.experimental import pallas as pl
from jax.experimental.pallas import tpu as pltpu
from jax.sharding import PartitionSpec as P

GROUP = 4


def shifted(block, levels, by):
    return lax.ppermute(block, "bands", [(z, (z + by) % levels) for z in range(levels)])


def halves(values):
    high = values.astype(jnp.bfloat16)
    return high, (values - high.astype(jnp.float32)).astype(jnp.bfloat16)


def product(rotation, accumulated, parts, classes, levels):
    members = levels // GROUP
    width = rotation.shape[0] // levels

    def kernel(rotation_ref, accumulated_ref, *refs):
        part_refs, out_ref = refs[:-1], refs[-1]
        z = lax.axis_index("bands")
        rows = []
        for c in classes:
            own = lax.rem(z + c + levels, GROUP)
            for m in range(members):
                start = pl.multiple_of((GROUP * m + own) * width, width)
                rows.append(rotation_ref[pl.ds(start, width), :])
        rot_high, rot_low = halves(jnp.concatenate(rows, 0))
        psi_high, psi_low = halves(jnp.concatenate([ref[...] for ref in part_refs], 0))
        left = jnp.concatenate([rot_high, rot_high, rot_low], 0)
        right = jnp.concatenate([psi_high, psi_low, psi_high], 0)
        out_ref[...] = accumulated_ref[...] + lax.dot_general(
            left, right, (((0,), (0,)), ((), ())), preferred_element_type=jnp.float32
        )

    rows, columns = accumulated.shape
    return pl.pallas_call(
        kernel,
        out_shape=jax.ShapeDtypeStruct((rows, columns), jnp.float32),
        compiler_params=pltpu.CompilerParams(vmem_limit_bytes=32 << 20),
        cost_estimate=pl.CostEstimate(
            flops=6 * rows * columns * rotation.shape[0], bytes_accessed=8 * rows * columns, transcendentals=0
        ),
        name="product",
    )(rotation, accumulated, *parts)


def solution(mesh):
    levels = mesh.shape["bands"]
    planes = mesh.shape["rows"]
    stride_groups = [[z + GROUP * m for m in range(levels // GROUP)] for z in range(GROUP)]

    def local(psi_panels, rotation, accumulated):
        copies = jnp.broadcast_to(rotation[None], (planes,) + rotation.shape)
        rot_whole = lax.all_to_all(copies, "rows", 0, 0).reshape(-1, rotation.shape[1])
        own = lax.all_gather(psi_panels.T, "bands", axis=0, tiled=True, axis_index_groups=stride_groups)
        own, rot_whole = lax.optimization_barrier((own, rot_whole))
        half = own.shape[0] // 2
        above = shifted(own, levels, -1)
        below = shifted(own, levels, 1)
        far_low = shifted(own[:half], levels, -2)
        far_high = shifted(own[half:], levels, 2)
        parts = (own, above, below, far_low, far_high)
        return product(rot_whole, accumulated.T, parts, (0, 1, -1, 2), levels).T

    spec = P("rows", "bands")
    return jax.shard_map(local, mesh=mesh, in_specs=(spec, spec, spec), out_specs=spec, check_vma=False)
```

time: 97.1 us -> 59.6 us (0.61)
  the two profiles are of different devices: /device:TPU:4 before, /device:TPU:66 now
where the time goes in v1:
time: 59.6 us; the launch traced here: 59.1 us
  blocking collectives  26.6 us (45%)
  starting transfers between devices  20.3 us (34%)
  waiting for transfers between devices  8.09 us (14%)
  Pallas kernels  2.35 us (4%)
  local copies, waits for them, and re-layouts  1.74 us (3%)
    all_gather x1, blocking collectives, local(): lax.all_gather(psi_panels.T, 'bands', axis=0, tiled=True, axis_index_grou...  26.6 us
    ppermute x4, starting transfers between devices, shifted(): lax.ppermute(block, 'bands', [(z, (z + by) % levels) for z in range(level...  12.6 us
    ppermute x4, waiting for transfers between devices, shifted(): lax.ppermute(block, 'bands', [(z, (z + by) % levels) for z in range(level...  8.09 us
    all_to_all x1, starting transfers between devices, local(): lax.all_to_all(copies, 'rows', 0, 0).reshape(-1, rotation.shape[1])  7.62 us
    pallas_call x1, Pallas kernels, product(): pl.pallas_call(kernel, out_shape=jax.ShapeDtypeStruct((rows, columns), jn...  2.35 us
    broadcast_in_dim x1, local copies, waits for them, and re-layouts, local(): copies = jnp.broadcast_to(rotation[None], (planes,) + rotation.shape)  1.72 us
  transfers between devices with their start and end apart: 5, of which 2 were waited for; matrix products, arithmetic and copies ran while one was open for 0% of the time, Pallas kernels for 0%

profile of v1, /device:TPU:66, one launch (start us, length us, event | category | flops | bytes accessed | tf_op | source)
XLA Modules:
  0.0 59.1 jit_solution(14044457138585371650)
XLA Ops:
  0.0 0.0 copy-start
  0.0 1.7 %broadcast_in_dim.2 = f32[32,8,500]{2,1,0:T(8,128)} broadcast(f32[8,500]{1,0:T(8,128)} %param.4), dimensions={1,2} | broadcast | bytes 528000 | tf_op jit(solution)/shard_map/broadcast_in_dim | solution.py:59
  1.7 7.6 %all-to-all-start = ((f32[32,8,500]{2,1,0:T(8,128)}), f32[32,8,500]{2,1,0:T(8,128)S(1)}, u32[]{:S(2)}, u32[]{:S(2)}) async-start(f32[32,8,500]{2,1,0:T(8,128)} %broadcast_in_dim.2), calls=%async_computation | async-start | bytes 1048576 | tf_op jit(solution)/shard_map/all_to_all | solution.py:60
  9.3 26.6 %all_gather.3.refs_0_ = f32[64,1024]{1,0:T(8,128)S(1)} all-gather(f32[16,1024]{1,0:T(8,128)} %bitcast.6), channel_id=1, replica_groups={{0,4,8,12},{1,5,9,13},{2,6,10,14},{3,7,11,15},{16,20,24,28},{17,21,25,2..., dimensions={0}, use_global_device_ids=true | all-gather | bytes 327680 | tf_op jit(solution)/shard_map/all_gather | solution.py:61
  36.0 0.0 all-to-all-done
  36.0 2.4 %collective-permute-start.1 = (f32[64,1024]{1,0:T(8,128)S(1)}, f32[64,1024]{1,0:T(8,128)S(1)}, u32[]{:S(2)}, u32[]{:S(2)}) collective-permute-start(f32[64,1024]{1,0:T(8,128)S(1)} %all_gather.3.refs_0_), channel_id=1, source_target_pairs={{0,1},{1,2},{2,3},{3,4},{4,5},{5,6},{6,7},{7,8},{8,9},{9,10},{10,1... | collective-permute-start | bytes 786440 | tf_op jit(solution)/shard_map/ppermute | solution.py:12
  38.4 3.4 %collective-permute-start = (f32[64,1024]{1,0:T(8,128)S(1)}, f32[64,1024]{1,0:T(8,128)S(1)}, u32[]{:S(2)}, u32[]{:S(2)}) collective-permute-start(f32[64,1024]{1,0:T(8,128)S(1)} %all_gather.3.refs_0_), channel_id=1, source_target_pairs={{0,15},{1,0},{2,1},{3,2},{4,3},{5,4},{6,5},{7,6},{8,7},{9,8},{10,9... | collective-permute-start | bytes 786440 | tf_op jit(solution)/shard_map/ppermute | solution.py:12
  41.9 4.9 %collective-permute-start.3 = (f32[32,1024]{1,0:T(8,128)S(1)}, f32[32,1024]{1,0:T(8,128)S(1)}, u32[]{:S(2)}, u32[]{:S(2)}) collective-permute-start(f32[32,1024]{1,0:T(8,128)S(1)} %get-tuple-element.9), channel_id=1, source_target_pairs={{0,2},{1,3},{2,4},{3,5},{4,6},{5,7},{6,8},{7,9},{8,10},{9,11},{10,... | collective-permute-start | bytes 393224 | tf_op jit(solution)/shard_map/ppermute | solution.py:12
  46.8 1.9 %collective-permute-start.2 = (f32[32,1024]{1,0:T(8,128)S(1)}, f32[32,1024]{1,0:T(8,128)S(1)}, u32[]{:S(2)}, u32[]{:S(2)}) collective-permute-start(f32[32,1024]{1,0:T(8,128)S(1)} %get-tuple-element.10), channel_id=1, source_target_pairs={{0,14},{1,15},{2,0},{3,1},{4,2},{5,3},{6,4},{7,5},{8,6},{9,7},{10,... | collective-permute-start | bytes 393224 | tf_op jit(solution)/shard_map/ppermute | solution.py:12
  48.7 1.0 %collective-permute-done.3.refs_4_ = f32[32,1024]{1,0:T(8,128)S(1)} collective-permute-done((f32[32,1024]{1,0:T(8,128)S(1)}, f32[32,1024]{1,0:T(8,128)S(1)}, u32[]{:S(2)}, u32[]{:S(2)}) %collective-permute-start.3) | collective-permute-done | bytes 131104 | tf_op jit(solution)/shard_map/ppermute | solution.py:12
  49.7 7.0 %collective-permute-done.2.refs_3_ = f32[32,1024]{1,0:T(8,128)S(1)} collective-permute-done((f32[32,1024]{1,0:T(8,128)S(1)}, f32[32,1024]{1,0:T(8,128)S(1)}, u32[]{:S(2)}, u32[]{:S(2)}) %collective-permute-start.2) | collective-permute-done | bytes 131104 | tf_op jit(solution)/shard_map/ppermute | solution.py:12
  56.8 0.0 collective-permute-done.1.refs_2_
  56.8 0.0 collective-permute-done.refs_1_
  56.8 0.0 copy-done
  56.8 2.3 %product.1 = f32[500,1024]{1,0:T(8,128)} custom-call(f32[256,500]{1,0:T(8,128)S(1)} %bitcast.4, f32[500,1024]{1,0:T(8,128)S(1)} %bitcast.5, f32[64,1024]{1,0:T(8,128)S(1)} %all_gather.3.refs_0_, f32[64,1024]{1,0:T(8,128)S(1)} %collective-permute-done.refs_1_, f32[64,1024]{1,0:T(8,128)S(1)} %collective-permute-done.1.refs_2_, ...), custom_call_target="tpu_custom_call" | custom-call | flops 786432000 | bytes 4096000 | tf_op jit(solution)/shard_map/product/pallas_call | solution.py:42
  (1 shorter events, 0.0 us)
Async XLA Ops:
  0.0 56.8 %copy-start = (f32[1024,500]{0,1:T(8,128)S(1)}, f32[1024,500]{0,1:T(8,128)}, u32[]{:S(2)}) copy-start(f32[1024,500]{0,1:T(8,128)} %param.5) | copy-start | bytes 6144004
  1.7 34.3 %all-to-all-start = ((f32[32,8,500]{2,1,0:T(8,128)}), f32[32,8,500]{2,1,0:T(8,128)S(1)}, u32[]{:S(2)}, u32[]{:S(2)}) async-start(f32[32,8,500]{2,1,0:T(8,128)} %broadcast_in_dim.2), calls=%async_computation | async-start | bytes 1048576 | tf_op jit(solution)/shard_map/all_to_all | solution.py:60
  36.0 20.8 %collective-permute-start.1 = (f32[64,1024]{1,0:T(8,128)S(1)}, f32[64,1024]{1,0:T(8,128)S(1)}, u32[]{:S(2)}, u32[]{:S(2)}) collective-permute-start(f32[64,1024]{1,0:T(8,128)S(1)} %all_gather.3.refs_0_), channel_id=1, source_target_pairs={{0,1},{1,2},{2,3},{3,4},{4,5},{5,6},{6,7},{7,8},{8,9},{9,10},{10,1... | collective-permute-start | bytes 786440 | tf_op jit(solution)/shard_map/ppermute | solution.py:12
  38.4 18.4 %collective-permute-start = (f32[64,1024]{1,0:T(8,128)S(1)}, f32[64,1024]{1,0:T(8,128)S(1)}, u32[]{:S(2)}, u32[]{:S(2)}) collective-permute-start(f32[64,1024]{1,0:T(8,128)S(1)} %all_gather.3.refs_0_), channel_id=1, source_target_pairs={{0,15},{1,0},{2,1},{3,2},{4,3},{5,4},{6,5},{7,6},{8,7},{9,8},{10,9... | collective-permute-start | bytes 786440 | tf_op jit(solution)/shard_map/ppermute | solution.py:12
  41.9 7.9 %collective-permute-start.3 = (f32[32,1024]{1,0:T(8,128)S(1)}, f32[32,1024]{1,0:T(8,128)S(1)}, u32[]{:S(2)}, u32[]{:S(2)}) collective-permute-start(f32[32,1024]{1,0:T(8,128)S(1)} %get-tuple-element.9), channel_id=1, source_target_pairs={{0,2},{1,3},{2,4},{3,5},{4,6},{5,7},{6,8},{7,9},{8,10},{9,11},{10,... | collective-permute-start | bytes 393224 | tf_op jit(solution)/shard_map/ppermute | solution.py:12
  46.8 10.0 %collective-permute-start.2 = (f32[32,1024]{1,0:T(8,128)S(1)}, f32[32,1024]{1,0:T(8,128)S(1)}, u32[]{:S(2)}, u32[]{:S(2)}) collective-permute-start(f32[32,1024]{1,0:T(8,128)S(1)} %get-tuple-element.10), channel_id=1, source_target_pairs={{0,14},{1,15},{2,0},{3,1},{4,2},{5,3},{6,4},{7,5},{8,6},{9,7},{10,... | collective-permute-start | bytes 393224 | tf_op jit(solution)/shard_map/ppermute | solution.py:12

commit v2 on v0

v2 whole, which is shorter than its diff:
```python
import jax
import jax.numpy as jnp
from jax import lax
from jax.experimental import pallas as pl
from jax.experimental.pallas import tpu as pltpu
from jax.sharding import PartitionSpec as P

GROUP = 4
TILE = 128


def halves(values):
    high = values.astype(jnp.bfloat16)
    return high, (values - high.astype(jnp.float32)).astype(jnp.bfloat16)


def left_operand(rows):
    high, low = halves(rows)
    return jnp.concatenate([high, high, low], 0).T


def right_operand(refs):
    high, low = halves(jnp.concatenate([ref[...] for ref in refs], 0))
    return jnp.concatenate([high, low, high], 0)


def cost(flops, moved):
    return pl.CostEstimate(flops=flops, bytes_accessed=moved, transcendentals=0)


def copies(block, count):
    def kernel(block_ref, out_ref, held, in_sem, out_sems):
        load = pltpu.make_async_copy(block_ref, held, in_sem)
        load.start()
        load.wait()
        stores = [pltpu.make_async_copy(held, out_ref.at[i], out_sems.at[i]) for i in range(count)]
        for store in stores:
            store.start()
        for store in stores:
            store.wait()

    return pl.pallas_call(
        kernel,
        out_shape=jax.ShapeDtypeStruct((count,) + block.shape, block.dtype),
        in_specs=[pl.BlockSpec(memory_space=pl.ANY)],
        out_specs=pl.BlockSpec(memory_space=pl.ANY),
        scratch_shapes=[
            pltpu.VMEM(block.shape, block.dtype),
            pltpu.SemaphoreType.DMA,
            pltpu.SemaphoreType.DMA((count,)),
        ],
        compiler_params=pltpu.CompilerParams(vmem_limit_bytes=8 << 20),
        cost_estimate=cost(0, count * block.size * 4),
        name="copies",
    )(block)


def prepare(rotation, levels, cores, ahead):
    members = levels // GROUP
    width = rotation.shape[0] // levels
    piece = width // cores
    columns = rotation.shape[1]

    def kernel(rotation_ref, early_ref, late_ref):
        z = lax.axis_index("bands")

        def rows(offsets):
            found = []
            for offset in offsets:
                own = lax.rem(z + offset + levels, GROUP)
                for m in range(members):
                    for core in range(cores):
                        at = core * levels + GROUP * m + own
                        found.append(rotation_ref[pl.ds(pl.multiple_of(at * piece, piece), piece), :])
            return jnp.concatenate(found, 0)

        early_ref[...] = left_operand(rows(ahead[0]))
        late_ref[...] = left_operand(rows(ahead[1]))

    return pl.pallas_call(
        kernel,
        out_shape=[jax.ShapeDtypeStruct((columns, 3 * len(o) * members * width), jnp.bfloat16) for o in ahead],
        compiler_params=pltpu.CompilerParams(vmem_limit_bytes=8 << 20),
        cost_estimate=cost(0, 5 * rotation.size * 4),
        name="prepare",
    )(rotation)


def add_part(left, total, parts):
    def kernel(left_ref, total_ref, *refs):
        refs[-1][...] = total_ref[...] + jnp.dot(
            left_ref[...], right_operand(refs[:-1]), preferred_element_type=jnp.float32
        )

    return pl.pallas_call(
        kernel,
        out_shape=jax.ShapeDtypeStruct(total.shape, jnp.float32),
        compiler_params=pltpu.CompilerParams(vmem_limit_bytes=20 << 20),
        cost_estimate=cost(2 * left.size * total.shape[1], 8 * total.size),
        name="add_part",
    )(left, total, *parts)


def add_last(left, total, parts):
    rows, columns = total.shape
    tiles = [(at, min(TILE, rows - at)) for at in range(0, rows, TILE)]

    def kernel(left_ref, total_ref, *refs):
        out_ref, held, sems = refs[-3:]
        right = right_operand(refs[:-3])
        stores = []
        for i, (at, size) in enumerate(tiles):
            held[at : at + size, :] = total_ref[at : at + size, :] + jnp.dot(
                left_ref[at : at + size, :], right, preferred_element_type=jnp.float32
            )
            stores.append(pltpu.make_async_copy(held.at[pl.ds(at, size)], out_ref.at[pl.ds(at, size)], sems.at[i]))
            stores[-1].start()
        for store in stores:
            store.wait()

    whole = pl.BlockSpec(memory_space=pltpu.VMEM)
    return pl.pallas_call(
        kernel,
        out_shape=jax.ShapeDtypeStruct(total.shape, jnp.float32),
        in_specs=[whole] * (2 + len(parts)),
        out_specs=pl.BlockSpec(memory_space=pl.ANY),
        scratch_shapes=[pltpu.VMEM((rows, columns), jnp.float32), pltpu.SemaphoreType.DMA((len(tiles),))],
        compiler_params=pltpu.CompilerParams(vmem_limit_bytes=20 << 20),
        cost_estimate=cost(2 * left.size * columns, 8 * total.size),
        name="add_last",
    )(left, total, *parts)


def solution(mesh):
    levels, planes = mesh.shape["bands"], mesh.shape["rows"]
    cores = 2
    chips = planes // cores
    same_core = [[cores * chip + core for chip in range(chips)] for core in range(cores)]
    same_chip = [[cores * chip + core for core in range(cores)] for chip in range(chips)]
    same_class = [[z + GROUP * m for m in range(levels // GROUP)] for z in range(GROUP)]

    def sent(block, by):
        pairs = [(i * levels + z, i * levels + (z + by(z)) % levels) for i in range(planes) for z in range(levels)]
        return lax.ppermute(block, ("rows", "bands"), pairs)

    def local(psi_panels, rotation, accumulated):
        spread = lax.all_to_all(copies(rotation, chips), "rows", 0, 0, axis_index_groups=same_core)
        spread = spread.reshape(-1, rotation.shape[1])
        own = lax.all_gather(psi_panels.T, "bands", axis=0, tiled=True, axis_index_groups=same_class)
        own, spread = lax.optimization_barrier((own, spread))
        above = sent(own, lambda z: -1)
        below = sent(own, lambda z: 1)
        across = sent(own, lambda z: 2 if z % 2 == 0 else -2)
        rot_whole = lax.all_gather(spread, "rows", axis=0, tiled=True, axis_index_groups=same_chip)
        early, late = prepare(rot_whole, levels, cores, ((0, 1, -1), (2,)))
        total = add_part(early, accumulated.T, (own, above, below))
        return add_last(late, total, (across,)).T

    spec = P("rows", "bands")
    return jax.shard_map(local, mesh=mesh, in_specs=(spec, spec, spec), out_specs=spec, check_vma=False)
```

time: 97.1 us -> 54.9 us (0.57)
  the two profiles are of different devices: /device:TPU:4 before, /device:TPU:2 now
where the time goes in v2:
time: 54.9 us; the launch traced here: 54.5 us
  blocking collectives  26.8 us (49%)
  starting transfers between devices  18.6 us (34%)
  waiting for transfers between devices  4.62 us (8%)
  Pallas kernels  3.7 us (7%)
  local copies, waits for them, and re-layouts  0.72 us (1%)
    all_gather x1, blocking collectives, local(): lax.all_gather(psi_panels.T, 'bands', axis=0, tiled=True, axis_index_grou...  24.7 us
    ppermute x3, starting transfers between devices, sent(): return lax.ppermute(block, ('rows', 'bands'), pairs)  9.29 us
    all_to_all x1, starting transfers between devices, local(): lax.all_to_all(copies(rotation, chips), 'rows', 0, 0, axis_index_groups=s...  9.26 us
    ppermute x3, waiting for transfers between devices, sent(): return lax.ppermute(block, ('rows', 'bands'), pairs)  4.62 us
    all_gather x1, blocking collectives, local(): lax.all_gather(spread, 'rows', axis=0, tiled=True, axis_index_groups=same...  2.18 us
    pallas_call x1, Pallas kernels, add_last(): pl.pallas_call(kernel, out_shape=jax.ShapeDtypeStruct(total.shape, jnp.fl...  1.56 us
  transfers between devices with their start and end apart: 4, of which 2 were waited for; matrix products, arithmetic and copies ran while one was open for 0% of the time, Pallas kernels for 2%

profile of v2, /device:TPU:2, one launch (start us, length us, event | category | flops | bytes accessed | tf_op | source)
XLA Modules:
  0.0 54.5 jit_solution(9585410604824584729)
XLA Ops:
  0.0 0.0 copy-start.1
  0.0 0.7 %copy-done.1 = f32[8,500]{1,0:T(8,128)S(1)} copy-done((f32[8,500]{1,0:T(8,128)S(1)}, f32[8,500]{1,0:T(8,128)}, u32[]{:S(2)}) %copy-start.1) | copy-done | bytes 16024
  0.7 0.0 copy-start
  0.7 0.8 %copies.1 = f32[16,8,500]{2,1,0:T(8,128)} custom-call(f32[8,500]{1,0:T(8,128)S(1)} %copy-done.1), custom_call_target="tpu_custom_call" | custom-call | bytes 256000 | tf_op jit(solution)/shard_map/copies/pallas_call | solution.py:42
  1.6 9.3 %all-to-all-start = ((f32[16,8,500]{2,1,0:T(8,128)}), f32[16,8,500]{2,1,0:T(8,128)S(1)}, u32[]{:S(2)}, u32[]{:S(2)}) async-start(f32[16,8,500]{2,1,0:T(8,128)} %copies.1), calls=%async_computation | async-start | bytes 524288 | tf_op jit(solution)/shard_map/all_to_all | solution.py:147
  10.8 24.7 %all_gather.6.refs_0_ = f32[64,1024]{1,0:T(8,128)S(1)} all-gather(f32[16,1024]{1,0:T(8,128)} %bitcast.6), channel_id=1, replica_groups={{0,4,8,12},{1,5,9,13},{2,6,10,14},{3,7,11,15},{16,20,24,28},{17,21,25,2..., dimensions={0}, use_global_device_ids=true | all-gather | bytes 327680 | tf_op jit(solution)/shard_map/all_gather | solution.py:149
  35.5 0.0 all-to-all-done
  35.5 3.0 %collective-permute-start.1 = (f32[64,1024]{1,0:T(8,128)S(1)}, f32[64,1024]{1,0:T(8,128)S(1)}, u32[]{:S(2)}, u32[]{:S(2)}) collective-permute-start(f32[64,1024]{1,0:T(8,128)S(1)} %all_gather.6.refs_0_), channel_id=1, source_target_pairs={{0,1},{1,2},{2,3},{3,4},{4,5},{5,6},{6,7},{7,8},{8,9},{9,10},{10,1... | collective-permute-start | bytes 786440 | tf_op jit(solution)/shard_map/ppermute | solution.py:144
  38.5 4.1 %collective-permute-start = (f32[64,1024]{1,0:T(8,128)S(1)}, f32[64,1024]{1,0:T(8,128)S(1)}, u32[]{:S(2)}, u32[]{:S(2)}) collective-permute-start(f32[64,1024]{1,0:T(8,128)S(1)} %all_gather.6.refs_0_), channel_id=1, source_target_pairs={{0,15},{1,0},{2,1},{3,2},{4,3},{5,4},{6,5},{7,6},{8,7},{9,8},{10,9... | collective-permute-start | bytes 786440 | tf_op jit(solution)/shard_map/ppermute | solution.py:144
  42.6 2.2 %collective-permute-start.2 = (f32[64,1024]{1,0:T(8,128)S(1)}, f32[64,1024]{1,0:T(8,128)S(1)}, u32[]{:S(2)}, u32[]{:S(2)}) collective-permute-start(f32[64,1024]{1,0:T(8,128)S(1)} %all_gather.6.refs_0_), channel_id=1, source_target_pairs={{0,2},{1,15},{2,4},{3,1},{4,6},{5,3},{6,8},{7,5},{8,10},{9,7},{10,... | collective-permute-start | bytes 786440 | tf_op jit(solution)/shard_map/ppermute | solution.py:144
  44.8 2.2 %all_gather.7.rotation_ref = f32[256,500]{1,0:T(8,128)S(1)} all-gather(f32[128,500]{1,0:T(8,128)S(1)} %bitcast.5), channel_id=1, replica_groups={{0,16},{32,48},{64,80},{96,112},{128,144},{160,176},{192,208},{224,240}..., dimensions={0}, use_global_device_ids=true | all-gather | bytes 768000 | tf_op jit(solution)/shard_map/all_gather | solution.py:154
  47.0 0.3 prepare.1
  47.3 0.0 collective-permute-done.1.refs_2_
  47.3 4.5 %collective-permute-done.refs_1_ = f32[64,1024]{1,0:T(8,128)S(1)} collective-permute-done((f32[64,1024]{1,0:T(8,128)S(1)}, f32[64,1024]{1,0:T(8,128)S(1)}, u32[]{:S(2)}, u32[]{:S(2)}) %collective-permute-start) | collective-permute-done | bytes 262176 | tf_op jit(solution)/shard_map/ppermute | solution.py:144
  51.8 0.0 copy-done
  51.8 1.0 %add_part.1.total_ref = f32[500,1024]{1,0:T(8,128)S(1)} custom-call(bf16[500,576]{1,0:T(8,128)(2,1)S(1)} %get-tuple-element.11.left_ref, f32[500,1024]{1,0:T(8,128)S(1)} %bitcast.4, f32[64,1024]{1,0:T(8,128)S(1)} %all_gather.6.refs_0_, f32[64,1024]{1,0:T(8,128)S(1)} %collective-permute-done.refs_1_, f32[64,1024]{1,0:T(8,128)S(1)} %collective-permute-done.1.refs_2_), custom_call_target="tpu_custom_call" | custom-call | flops 589824000 | bytes 4096000 | tf_op jit(solution)/shard_map/add_part/pallas_call | solution.py:95
  52.8 0.1 collective-permute-done.2.refs_0_
  52.9 1.6 %add_last.1 = f32[500,1024]{1,0:T(8,128)} custom-call(bf16[500,192]{1,0:T(8,128)(2,1)S(1)} %get-tuple-element.10.left_ref, f32[500,1024]{1,0:T(8,128)S(1)} %add_part.1.total_ref, f32[64,1024]{1,0:T(8,128)S(1)} %collective-permute-done.2.refs_0_), custom_call_target="tpu_custom_call" | custom-call | flops 196608000 | bytes 4096000 | tf_op jit(solution)/shard_map/add_last/pallas_call | solution.py:122
Async XLA Ops:
  0.0 0.7 %copy-start.1 = (f32[8,500]{1,0:T(8,128)S(1)}, f32[8,500]{1,0:T(8,128)}, u32[]{:S(2)}) copy-start(f32[8,500]{1,0:T(8,128)} %block_ref.1) | copy-start | bytes 48004
  0.7 51.1 %copy-start = (f32[1024,500]{0,1:T(8,128)S(1)}, f32[1024,500]{0,1:T(8,128)}, u32[]{:S(2)}) copy-start(f32[1024,500]{0,1:T(8,128)} %param.5) | copy-start | bytes 6144004
  1.6 33.9 %all-to-all-start = ((f32[16,8,500]{2,1,0:T(8,128)}), f32[16,8,500]{2,1,0:T(8,128)S(1)}, u32[]{:S(2)}, u32[]{:S(2)}) async-start(f32[16,8,500]{2,1,0:T(8,128)} %copies.1), calls=%async_computation | async-start | bytes 524288 | tf_op jit(solution)/shard_map/all_to_all | solution.py:147
  35.5 11.8 %collective-permute-start.1 = (f32[64,1024]{1,0:T(8,128)S(1)}, f32[64,1024]{1,0:T(8,128)S(1)}, u32[]{:S(2)}, u32[]{:S(2)}) collective-permute-start(f32[64,1024]{1,0:T(8,128)S(1)} %all_gather.6.refs_0_), channel_id=1, source_target_pairs={{0,1},{1,2},{2,3},{3,4},{4,5},{5,6},{6,7},{7,8},{8,9},{9,10},{10,1... | collective-permute-start | bytes 786440 | tf_op jit(solution)/shard_map/ppermute | solution.py:144
  38.5 13.3 %collective-permute-start = (f32[64,1024]{1,0:T(8,128)S(1)}, f32[64,1024]{1,0:T(8,128)S(1)}, u32[]{:S(2)}, u32[]{:S(2)}) collective-permute-start(f32[64,1024]{1,0:T(8,128)S(1)} %all_gather.6.refs_0_), channel_id=1, source_target_pairs={{0,15},{1,0},{2,1},{3,2},{4,3},{5,4},{6,5},{7,6},{8,7},{9,8},{10,9... | collective-permute-start | bytes 786440 | tf_op jit(solution)/shard_map/ppermute | solution.py:144
  42.6 10.4 %collective-permute-start.2 = (f32[64,1024]{1,0:T(8,128)S(1)}, f32[64,1024]{1,0:T(8,128)S(1)}, u32[]{:S(2)}, u32[]{:S(2)}) collective-permute-start(f32[64,1024]{1,0:T(8,128)S(1)} %all_gather.6.refs_0_), channel_id=1, source_target_pairs={{0,2},{1,15},{2,4},{3,1},{4,6},{5,3},{6,8},{7,5},{8,10},{9,7},{10,... | collective-permute-start | bytes 786440 | tf_op jit(solution)/shard_map/ppermute | solution.py:144

commit v3 on v2

--- a/solution.py
+++ b/solution.py
@@ -5,8 +5,11 @@
 from jax.experimental.pallas import tpu as pltpu
 from jax.sharding import PartitionSpec as P
 
-GROUP = 4
 TILE = 128
+LONG = 10**11
+
+HELD = ((0, 0), (3, -3), (4, -4), (7, -7))
+FROM = ((0, 0), (1, 1), (-1, -1), (2, -2))
 
 
 def halves(values):
@@ -50,13 +53,28 @@
             pltpu.SemaphoreType.DMA((count,)),
         ],
         compiler_params=pltpu.CompilerParams(vmem_limit_bytes=8 << 20),
-        cost_estimate=cost(0, count * block.size * 4),
+        cost_estimate=cost(LONG, count * block.size * 4),
         name="copies",
     )(block)
 
 
-def prepare(rotation, levels, cores, ahead):
-    members = levels // GROUP
+def stacked(blocks):
+    rows, columns = blocks[0].shape
+
+    def kernel(*refs):
+        for i, ref in enumerate(refs[:-1]):
+            refs[-1][rows * i : rows * (i + 1), :] = ref[...]
+
+    return pl.pallas_call(
+        kernel,
+        out_shape=jax.ShapeDtypeStruct((rows * len(blocks), columns), blocks[0].dtype),
+        compiler_params=pltpu.CompilerParams(vmem_limit_bytes=8 << 20),
+        cost_estimate=cost(LONG, 8 * rows * columns * len(blocks)),
+        name="stacked",
+    )(*blocks)
+
+
+def prepare(rotation, levels, cores, sources):
     width = rotation.shape[0] // levels
     piece = width // cores
     columns = rotation.shape[1]
@@ -64,22 +82,29 @@
     def kernel(rotation_ref, early_ref, late_ref):
         z = lax.axis_index("bands")
 
-        def rows(offsets):
+        def moved(level, offsets):
+            even, odd = offsets
+            return lax.rem(level + jnp.where(lax.rem(level, 2) == 0, even, odd) + levels, levels)
+
+        def rows(part):
             found = []
-            for offset in offsets:
-                own = lax.rem(z + offset + levels, GROUP)
-                for m in range(members):
+            for source in part:
+                holder = moved(z, source)
+                for offsets in HELD:
+                    level = moved(holder, offsets)
                     for core in range(cores):
-                        at = core * levels + GROUP * m + own
-                        found.append(rotation_ref[pl.ds(pl.multiple_of(at * piece, piece), piece), :])
+                        at = pl.multiple_of((core * levels + level) * piece, piece)
+                        found.append(rotation_ref[pl.ds(at, piece), :])
             return jnp.concatenate(found, 0)
 
-        early_ref[...] = left_operand(rows(ahead[0]))
-        late_ref[...] = left_operand(rows(ahead[1]))
+        early_ref[...] = left_operand(rows(sources[0]))
+        late_ref[...] = left_operand(rows(sources[1]))
 
     return pl.pallas_call(
         kernel,
-        out_shape=[jax.ShapeDtypeStruct((columns, 3 * len(o) * members * width), jnp.bfloat16) for o in ahead],
+        out_shape=[
+            jax.ShapeDtypeStruct((columns, 3 * len(part) * len(HELD) * width), jnp.bfloat16) for part in sources
+        ],
         compiler_params=pltpu.CompilerParams(vmem_limit_bytes=8 << 20),
         cost_estimate=cost(0, 5 * rotation.size * 4),
         name="prepare",
@@ -137,22 +162,21 @@
     chips = planes // cores
     same_core = [[cores * chip + core for chip in range(chips)] for core in range(cores)]
     same_chip = [[cores * chip + core for core in range(cores)] for chip in range(chips)]
-    same_class = [[z + GROUP * m for m in range(levels // GROUP)] for z in range(GROUP)]
 
-    def sent(block, by):
-        pairs = [(i * levels + z, i * levels + (z + by(z)) % levels) for i in range(planes) for z in range(levels)]
+    def fetched(block, offsets):
+        pairs = [
+            (i * levels + (z + offsets[z % 2]) % levels, i * levels + z) for i in range(planes) for z in range(levels)
+        ]
         return lax.ppermute(block, ("rows", "bands"), pairs)
 
     def local(psi_panels, rotation, accumulated):
         spread = lax.all_to_all(copies(rotation, chips), "rows", 0, 0, axis_index_groups=same_core)
         spread = spread.reshape(-1, rotation.shape[1])
-        own = lax.all_gather(psi_panels.T, "bands", axis=0, tiled=True, axis_index_groups=same_class)
-        own, spread = lax.optimization_barrier((own, spread))
-        above = sent(own, lambda z: -1)
-        below = sent(own, lambda z: 1)
-        across = sent(own, lambda z: 2 if z % 2 == 0 else -2)
+        psi = psi_panels.T
+        own = stacked([psi] + [fetched(psi, offsets) for offsets in HELD[1:]])
+        above, below, across = [fetched(own, offsets) for offsets in FROM[1:]]
         rot_whole = lax.all_gather(spread, "rows", axis=0, tiled=True, axis_index_groups=same_chip)
-        early, late = prepare(rot_whole, levels, cores, ((0, 1, -1), (2,)))
+        early, late = prepare(rot_whole, levels, cores, (FROM[:3], FROM[3:]))
         total = add_part(early, accumulated.T, (own, above, below))
         return add_last(late, total, (across,)).T
 

time: 54.9 us -> 50.5 us (0.920)
  the two profiles are of different devices: /device:TPU:2 before, /device:TPU:22 now
where the time goes in v3:
time: 50.5 us; the launch traced here: 50 us
  starting transfers between devices  41.3 us (82%)
  Pallas kernels  3.73 us (7%)
  blocking collectives  2.18 us (4%)
  waiting for transfers between devices  1.97 us (4%)
  local copies, waits for them, and re-layouts  0.72 us (1%)
    ppermute x6, starting transfers between devices, fetched(): return lax.ppermute(block, ('rows', 'bands'), pairs)  34.1 us
    all_to_all x1, starting transfers between devices, local(): lax.all_to_all(copies(rotation, chips), 'rows', 0, 0, axis_index_groups=s...  7.21 us
    all_gather x1, blocking collectives, local(): lax.all_gather(spread, 'rows', axis=0, tiled=True, axis_index_groups=same...  2.18 us
    ppermute x6, waiting for transfers between devices, fetched(): return lax.ppermute(block, ('rows', 'bands'), pairs)  1.97 us
    pallas_call x1, Pallas kernels, add_last(): pl.pallas_call(kernel, out_shape=jax.ShapeDtypeStruct(total.shape, jnp.fl...  1.56 us
  transfers between devices with their start and end apart: 7, of which 1 were waited for; matrix products, arithmetic and copies ran while one was open for 0% of the time, Pallas kernels for 4%

profile of v3, /device:TPU:22, one launch (start us, length us, event | category | flops | bytes accessed | tf_op | source)
XLA Modules:
  0.0 50.0 jit_solution(2839247904745745729)
XLA Ops:
  0.0 0.0 copy-start.1
  0.0 13.3 %collective-permute-start.2 = (f32[16,1024]{1,0:T(8,128)}, f32[16,1024]{1,0:T(8,128)S(1)}, u32[]{:S(2)}, u32[]{:S(2)}) collective-permute-start(f32[16,1024]{1,0:T(8,128)} %bitcast.5), channel_id=1, source_target_pairs={{7,0},{10,1},{9,2},{12,3},{11,4},{14,5},{13,6},{0,7},{15,8},{2,9},... | collective-permute-start | bytes 196616 | tf_op jit(solution)/shard_map/ppermute | solution.py:170
  13.3 1.9 %collective-permute-start.1 = (f32[16,1024]{1,0:T(8,128)}, f32[16,1024]{1,0:T(8,128)S(1)}, u32[]{:S(2)}, u32[]{:S(2)}) collective-permute-start(f32[16,1024]{1,0:T(8,128)} %bitcast.6), channel_id=1, source_target_pairs={{4,0},{13,1},{6,2},{15,3},{8,4},{1,5},{10,6},{3,7},{12,8},{5,9},{1... | collective-permute-start | bytes 196616 | tf_op jit(solution)/shard_map/ppermute | solution.py:170
  15.2 4.7 %collective-permute-start = (f32[16,1024]{1,0:T(8,128)}, f32[16,1024]{1,0:T(8,128)S(1)}, u32[]{:S(2)}, u32[]{:S(2)}) collective-permute-start(f32[16,1024]{1,0:T(8,128)} %bitcast.7), channel_id=1, source_target_pairs={{3,0},{14,1},{5,2},{0,3},{7,4},{2,5},{9,6},{4,7},{11,8},{6,9},{13,... | collective-permute-start | bytes 196616 | tf_op jit(solution)/shard_map/ppermute | solution.py:170
  20.0 0.0 copy-start.2
  20.0 0.7 %copy-done.2 = f32[8,500]{1,0:T(8,128)S(1)} copy-done((f32[8,500]{1,0:T(8,128)S(1)}, f32[8,500]{1,0:T(8,128)}, u32[]{:S(2)}) %copy-start.2) | copy-done | bytes 16024
  20.7 0.8 %copies.1 = f32[16,8,500]{2,1,0:T(8,128)} custom-call(f32[8,500]{1,0:T(8,128)S(1)} %copy-done.2), custom_call_target="tpu_custom_call" | custom-call | flops 99999997952 | bytes 256000 | tf_op jit(solution)/shard_map/copies/pallas_call | solution.py:45
  21.5 7.2 %all-to-all-start = ((f32[16,8,500]{2,1,0:T(8,128)}), f32[16,8,500]{2,1,0:T(8,128)S(1)}, u32[]{:S(2)}, u32[]{:S(2)}) async-start(f32[16,8,500]{2,1,0:T(8,128)} %copies.1), calls=%async_computation | async-start | bytes 524288 | tf_op jit(solution)/shard_map/all_to_all | solution.py:173
  28.7 0.0 collective-permute-done.2.refs_3_
  28.8 0.0 collective-permute-done.1.refs_2_
  28.8 0.0 collective-permute-done.refs_1_
  28.8 0.0 copy-done.1
  28.8 0.0 copy-start
  28.8 4.7 %collective-permute-start.4 = (f32[64,1024]{1,0:T(8,128)S(1)}, f32[64,1024]{1,0:T(8,128)S(1)}, u32[]{:S(2)}, u32[]{:S(2)}) collective-permute-start(f32[64,1024]{1,0:T(8,128)S(1)} %stacked.1.refs_0_), channel_id=1, source_target_pairs={{15,0},{0,1},{1,2},{2,3},{3,4},{4,5},{5,6},{6,7},{7,8},{8,9},{9,10... | collective-permute-start | bytes 786440 | tf_op jit(solution)/shard_map/ppermute | solution.py:170
  33.6 3.8 %collective-permute-start.3 = (f32[64,1024]{1,0:T(8,128)S(1)}, f32[64,1024]{1,0:T(8,128)S(1)}, u32[]{:S(2)}, u32[]{:S(2)}) collective-permute-start(f32[64,1024]{1,0:T(8,128)S(1)} %stacked.1.refs_0_), channel_id=1, source_target_pairs={{1,0},{2,1},{3,2},{4,3},{5,4},{6,5},{7,6},{8,7},{9,8},{10,9},{11,1... | collective-permute-start | bytes 786440 | tf_op jit(solution)/shard_map/ppermute | solution.py:170
  37.4 5.6 %collective-permute-start.5 = (f32[64,1024]{1,0:T(8,128)S(1)}, f32[64,1024]{1,0:T(8,128)S(1)}, u32[]{:S(2)}, u32[]{:S(2)}) collective-permute-start(f32[64,1024]{1,0:T(8,128)S(1)} %stacked.1.refs_0_), channel_id=1, source_target_pairs={{2,0},{15,1},{4,2},{1,3},{6,4},{3,5},{8,6},{5,7},{10,8},{7,9},{12,... | collective-permute-start | bytes 786440 | tf_op jit(solution)/shard_map/ppermute | solution.py:170
  43.0 0.0 all-to-all-done
  43.0 2.2 %all_gather.3.rotation_ref = f32[256,500]{1,0:T(8,128)S(1)} all-gather(f32[128,500]{1,0:T(8,128)S(1)} %bitcast.9), channel_id=1, replica_groups={{0,16},{32,48},{64,80},{96,112},{128,144},{160,176},{192,208},{224,240}..., dimensions={0}, use_global_device_ids=true | all-gather | bytes 768000 | tf_op jit(solution)/shard_map/all_gather | solution.py:178
  45.2 0.3 prepare.1
  45.5 0.0 collective-permute-done.4.refs_2_
  45.5 0.0 collective-permute-done.3.refs_1_
  45.5 0.0 copy-done
  45.5 1.0 %add_part.1.total_ref = f32[500,1024]{1,0:T(8,128)S(1)} custom-call(bf16[500,576]{1,0:T(8,128)(2,1)S(1)} %get-tuple-element.8.left_ref, f32[500,1024]{1,0:T(8,128)S(1)} %bitcast.4, f32[64,1024]{1,0:T(8,128)S(1)} %stacked.1.refs_0_, f32[64,1024]{1,0:T(8,128)S(1)} %collective-permute-done.3.refs_1_, f32[64,1024]{1,0:T(8,128)S(1)} %collective-permute-done.4.refs_2_), custom_call_target="tpu_custom_call" | custom-call | flops 589824000 | bytes 4096000 | tf_op jit(solution)/shard_map/add_part/pallas_call | solution.py:120
  46.5 2.0 %collective-permute-done.5.refs_0_ = f32[64,1024]{1,0:T(8,128)S(1)} collective-permute-done((f32[64,1024]{1,0:T(8,128)S(1)}, f32[64,1024]{1,0:T(8,128)S(1)}, u32[]{:S(2)}, u32[]{:S(2)}) %collective-permute-start.5) | collective-permute-done | bytes 262176 | tf_op jit(solution)/shard_map/ppermute | solution.py:170
  48.5 1.6 %add_last.1 = f32[500,1024]{1,0:T(8,128)} custom-call(bf16[500,192]{1,0:T(8,128)(2,1)S(1)} %get-tuple-element.7.left_ref, f32[500,1024]{1,0:T(8,128)S(1)} %add_part.1.total_ref, f32[64,1024]{1,0:T(8,128)S(1)} %collective-permute-done.5.refs_0_), custom_call_target="tpu_custom_call" | custom-call | flops 196608000 | bytes 4096000 | tf_op jit(solution)/shard_map/add_last/pallas_call | solution.py:147
  (1 shorter events, 0.0 us)
Async XLA Ops:
  0.0 28.8 %copy-start.1 = (f32[1024,16]{0,1:T(8,128)S(1)}, f32[1024,16]{0,1:T(8,128)}, u32[]{:S(2)}) copy-start(f32[1024,16]{0,1:T(8,128)} %param.3) | copy-start | bytes 196612
  0.0 28.7 %collective-permute-start.2 = (f32[16,1024]{1,0:T(8,128)}, f32[16,1024]{1,0:T(8,128)S(1)}, u32[]{:S(2)}, u32[]{:S(2)}) collective-permute-start(f32[16,1024]{1,0:T(8,128)} %bitcast.5), channel_id=1, source_target_pairs={{7,0},{10,1},{9,2},{12,3},{11,4},{14,5},{13,6},{0,7},{15,8},{2,9},... | collective-permute-start | bytes 196616 | tf_op jit(solution)/shard_map/ppermute | solution.py:170
  13.3 15.5 %collective-permute-start.1 = (f32[16,1024]{1,0:T(8,128)}, f32[16,1024]{1,0:T(8,128)S(1)}, u32[]{:S(2)}, u32[]{:S(2)}) collective-permute-start(f32[16,1024]{1,0:T(8,128)} %bitcast.6), channel_id=1, source_target_pairs={{4,0},{13,1},{6,2},{15,3},{8,4},{1,5},{10,6},{3,7},{12,8},{5,9},{1... | collective-permute-start | bytes 196616 | tf_op jit(solution)/shard_map/ppermute | solution.py:170
  15.2 13.6 %collective-permute-start = (f32[16,1024]{1,0:T(8,128)}, f32[16,1024]{1,0:T(8,128)S(1)}, u32[]{:S(2)}, u32[]{:S(2)}) collective-permute-start(f32[16,1024]{1,0:T(8,128)} %bitcast.7), channel_id=1, source_target_pairs={{3,0},{14,1},{5,2},{0,3},{7,4},{2,5},{9,6},{4,7},{11,8},{6,9},{13,... | collective-permute-start | bytes 196616 | tf_op jit(solution)/shard_map/ppermute | solution.py:170
  20.0 0.7 %copy-start.2 = (f32[8,500]{1,0:T(8,128)S(1)}, f32[8,500]{1,0:T(8,128)}, u32[]{:S(2)}) copy-start(f32[8,500]{1,0:T(8,128)} %block_ref.1) | copy-start | bytes 48004
  21.5 21.4 %all-to-all-start = ((f32[16,8,500]{2,1,0:T(8,128)}), f32[16,8,500]{2,1,0:T(8,128)S(1)}, u32[]{:S(2)}, u32[]{:S(2)}) async-start(f32[16,8,500]{2,1,0:T(8,128)} %copies.1), calls=%async_computation | async-start | bytes 524288 | tf_op jit(solution)/shard_map/all_to_all | solution.py:173
  28.8 16.7 %copy-start = (f32[1024,500]{0,1:T(8,128)S(1)}, f32[1024,500]{0,1:T(8,128)}, u32[]{:S(2)}) copy-start(f32[1024,500]{0,1:T(8,128)} %param.5) | copy-start | bytes 6144004
  28.8 16.7 %collective-permute-start.4 = (f32[64,1024]{1,0:T(8,128)S(1)}, f32[64,1024]{1,0:T(8,128)S(1)}, u32[]{:S(2)}, u32[]{:S(2)}) collective-permute-start(f32[64,1024]{1,0:T(8,128)S(1)} %stacked.1.refs_0_), channel_id=1, source_target_pairs={{15,0},{0,1},{1,2},{2,3},{3,4},{4,5},{5,6},{6,7},{7,8},{8,9},{9,10... | collective-permute-start | bytes 786440 | tf_op jit(solution)/shard_map/ppermute | solution.py:170
  33.6 11.9 %collective-permute-start.3 = (f32[64,1024]{1,0:T(8,128)S(1)}, f32[64,1024]{1,0:T(8,128)S(1)}, u32[]{:S(2)}, u32[]{:S(2)}) collective-permute-start(f32[64,1024]{1,0:T(8,128)S(1)} %stacked.1.refs_0_), channel_id=1, source_target_pairs={{1,0},{2,1},{3,2},{4,3},{5,4},{6,5},{7,6},{8,7},{9,8},{10,9},{11,1... | collective-permute-start | bytes 786440 | tf_op jit(solution)/shard_map/ppermute | solution.py:170
  37.4 11.1 %collective-permute-start.5 = (f32[64,1024]{1,0:T(8,128)S(1)}, f32[64,1024]{1,0:T(8,128)S(1)}, u32[]{:S(2)}, u32[]{:S(2)}) collective-permute-start(f32[64,1024]{1,0:T(8,128)S(1)} %stacked.1.refs_0_), channel_id=1, source_target_pairs={{2,0},{15,1},{4,2},{1,3},{6,4},{3,5},{8,6},{5,7},{10,8},{7,9},{12,... | collective-permute-start | bytes 786440 | tf_op jit(solution)/shard_map/ppermute | solution.py:170

commit v4 on v3

--- a/solution.py
+++ b/solution.py
@@ -8,8 +8,10 @@
 TILE = 128
 LONG = 10**11
 
-HELD = ((0, 0), (3, -3), (4, -4), (7, -7))
-FROM = ((0, 0), (1, 1), (-1, -1), (2, -2))
+PAIR = 3
+HOP = (4, -4)
+HELD = ((0, -3), (3, 0), (4, -7), (7, -4))
+FROM = ((0, 0), (-1, -1), (2, -2), (1, 1))
 
 
 def halves(values):
@@ -32,11 +34,8 @@
 
 
 def copies(block, count):
-    def kernel(block_ref, out_ref, held, in_sem, out_sems):
-        load = pltpu.make_async_copy(block_ref, held, in_sem)
-        load.start()
-        load.wait()
-        stores = [pltpu.make_async_copy(held, out_ref.at[i], out_sems.at[i]) for i in range(count)]
+    def kernel(block_ref, out_ref, sems):
+        stores = [pltpu.make_async_copy(block_ref, out_ref.at[i], sems.at[i]) for i in range(count)]
         for store in stores:
             store.start()
         for store in stores:
@@ -45,13 +44,9 @@
     return pl.pallas_call(
         kernel,
         out_shape=jax.ShapeDtypeStruct((count,) + block.shape, block.dtype),
-        in_specs=[pl.BlockSpec(memory_space=pl.ANY)],
+        in_specs=[pl.BlockSpec(memory_space=pltpu.VMEM)],
         out_specs=pl.BlockSpec(memory_space=pl.ANY),
-        scratch_shapes=[
-            pltpu.VMEM(block.shape, block.dtype),
-            pltpu.SemaphoreType.DMA,
-            pltpu.SemaphoreType.DMA((count,)),
-        ],
+        scratch_shapes=[pltpu.SemaphoreType.DMA((count,))],
         compiler_params=pltpu.CompilerParams(vmem_limit_bytes=8 << 20),
         cost_estimate=cost(LONG, count * block.size * 4),
         name="copies",
@@ -172,13 +167,14 @@
     def local(psi_panels, rotation, accumulated):
         spread = lax.all_to_all(copies(rotation, chips), "rows", 0, 0, axis_index_groups=same_core)
         spread = spread.reshape(-1, rotation.shape[1])
-        psi = psi_panels.T
-        own = stacked([psi] + [fetched(psi, offsets) for offsets in HELD[1:]])
-        above, below, across = [fetched(own, offsets) for offsets in FROM[1:]]
+        pairs = [[z, (z + PAIR) % levels] for z in range(0, levels, 2)]
+        couple = lax.all_gather(psi_panels.T, "bands", axis=0, tiled=True, axis_index_groups=pairs)
+        own = stacked([couple, fetched(couple, HOP)])
+        below, across, above = [fetched(own, offsets) for offsets in FROM[1:]]
         rot_whole = lax.all_gather(spread, "rows", axis=0, tiled=True, axis_index_groups=same_chip)
         early, late = prepare(rot_whole, levels, cores, (FROM[:3], FROM[3:]))
-        total = add_part(early, accumulated.T, (own, above, below))
-        return add_last(late, total, (across,)).T
+        total = add_part(early, accumulated.T, (own, below, across))
+        return add_last(late, total, (above,)).T
 
     spec = P("rows", "bands")
     return jax.shard_map(local, mesh=mesh, in_specs=(spec, spec, spec), out_specs=spec, check_vma=False)

time: 50.5 us -> 48.7 us (0.964)
  the two profiles are of different devices: /device:TPU:22 before, /device:TPU:1 now
where the time goes in v4:
time: 48.7 us; the launch traced here: 48.2 us
  starting transfers between devices  31.9 us (66%)
  blocking collectives  11.8 us (24%)
  Pallas kernels  3.72 us (8%)
  local copies, waits for them, and re-layouts  0.72 us (1%)
    ppermute x4, starting transfers between devices, fetched(): return lax.ppermute(block, ('rows', 'bands'), pairs)  25.1 us
    all_gather x1, blocking collectives, local(): lax.all_gather(psi_panels.T, 'bands', axis=0, tiled=True, axis_index_grou...  7.75 us
    all_to_all x1, starting transfers between devices, local(): lax.all_to_all(copies(rotation, chips), 'rows', 0, 0, axis_index_groups=s...  6.77 us
    all_gather x1, blocking collectives, local(): lax.all_gather(spread, 'rows', axis=0, tiled=True, axis_index_groups=same...  4.05 us
    pallas_call x1, Pallas kernels, add_last(): pl.pallas_call(kernel, out_shape=jax.ShapeDtypeStruct(total.shape, jnp.fl...  1.56 us
    pallas_call x1, Pallas kernels, add_part(): pl.pallas_call(kernel, out_shape=jax.ShapeDtypeStruct(total.shape, jnp.fl...  0.99 us
  transfers between devices with their start and end apart: 5, of which 0 were waited for; matrix products, arithmetic and copies ran while one was open for 0% of the time, Pallas kernels for 4%

profile of v4, /device:TPU:1, one launch (start us, length us, event | category | flops | bytes accessed | tf_op | source)
XLA Modules:
  0.0 48.2 jit_solution(5551249132985213178)
XLA Ops:
  0.0 7.7 %all_gather.7.refs_0_ = f32[32,1024]{1,0:T(8,128)S(1)} all-gather(f32[16,1024]{1,0:T(8,128)} %bitcast.6), channel_id=1, replica_groups={{0,3},{2,5},{4,7},{6,9},{8,11},{10,13},{12,15},{14,1},{16,19},{18,21},{..., dimensions={0}, use_global_device_ids=true | all-gather | bytes 196608 | tf_op jit(solution)/shard_map/all_gather | solution.py:171
  7.7 11.4 %collective-permute-start = (f32[32,1024]{1,0:T(8,128)S(1)}, f32[32,1024]{1,0:T(8,128)S(1)}, u32[]{:S(2)}, u32[]{:S(2)}) collective-permute-start(f32[32,1024]{1,0:T(8,128)S(1)} %all_gather.7.refs_0_), channel_id=1, source_target_pairs={{4,0},{13,1},{6,2},{15,3},{8,4},{1,5},{10,6},{3,7},{12,8},{5,9},{1... | collective-permute-start | bytes 393224 | tf_op jit(solution)/shard_map/ppermute | solution.py:165
  19.1 0.0 copy-start.1
  19.1 0.7 %copy-done.1 = f32[8,500]{1,0:T(8,128)S(1)} copy-done((f32[8,500]{1,0:T(8,128)S(1)}, f32[8,500]{1,0:T(8,128)}, u32[]{:S(2)}) %copy-start.1) | copy-done | bytes 16024
  19.8 0.8 %copies.1 = f32[16,8,500]{2,1,0:T(8,128)} custom-call(f32[8,500]{1,0:T(8,128)S(1)} %copy-done.1), custom_call_target="tpu_custom_call" | custom-call | flops 99999997952 | bytes 256000 | tf_op jit(solution)/shard_map/copies/pallas_call | solution.py:44
  20.7 6.8 %all-to-all-start = ((f32[16,8,500]{2,1,0:T(8,128)}), f32[16,8,500]{2,1,0:T(8,128)S(1)}, u32[]{:S(2)}, u32[]{:S(2)}) async-start(f32[16,8,500]{2,1,0:T(8,128)} %copies.1), calls=%async_computation | async-start | bytes 524288 | tf_op jit(solution)/shard_map/all_to_all | solution.py:168
  27.4 0.0 collective-permute-done.refs_1_
  27.4 0.0 copy-start
  27.5 7.2 %collective-permute-start.2 = (f32[64,1024]{1,0:T(8,128)S(1)}, f32[64,1024]{1,0:T(8,128)S(1)}, u32[]{:S(2)}, u32[]{:S(2)}) collective-permute-start(f32[64,1024]{1,0:T(8,128)S(1)} %stacked.1.refs_0_), channel_id=1, source_target_pairs={{2,0},{15,1},{4,2},{1,3},{6,4},{3,5},{8,6},{5,7},{10,8},{7,9},{12,... | collective-permute-start | bytes 786440 | tf_op jit(solution)/shard_map/ppermute | solution.py:165
  34.7 1.9 %collective-permute-start.1 = (f32[64,1024]{1,0:T(8,128)S(1)}, f32[64,1024]{1,0:T(8,128)S(1)}, u32[]{:S(2)}, u32[]{:S(2)}) collective-permute-start(f32[64,1024]{1,0:T(8,128)S(1)} %stacked.1.refs_0_), channel_id=1, source_target_pairs={{15,0},{0,1},{1,2},{2,3},{3,4},{4,5},{5,6},{6,7},{7,8},{8,9},{9,10... | collective-permute-start | bytes 786440 | tf_op jit(solution)/shard_map/ppermute | solution.py:165
  36.7 4.6 %collective-permute-start.3 = (f32[64,1024]{1,0:T(8,128)S(1)}, f32[64,1024]{1,0:T(8,128)S(1)}, u32[]{:S(2)}, u32[]{:S(2)}) collective-permute-start(f32[64,1024]{1,0:T(8,128)S(1)} %stacked.1.refs_0_), channel_id=1, source_target_pairs={{1,0},{2,1},{3,2},{4,3},{5,4},{6,5},{7,6},{8,7},{9,8},{10,9},{11,1... | collective-permute-start | bytes 786440 | tf_op jit(solution)/shard_map/ppermute | solution.py:165
  41.3 0.0 all-to-all-done
  41.3 4.1 %all_gather.6.rotation_ref = f32[256,500]{1,0:T(8,128)S(1)} all-gather(f32[128,500]{1,0:T(8,128)S(1)} %bitcast.5), channel_id=1, replica_groups={{0,16},{32,48},{64,80},{96,112},{128,144},{160,176},{192,208},{224,240}..., dimensions={0}, use_global_device_ids=true | all-gather | bytes 768000 | tf_op jit(solution)/shard_map/all_gather | solution.py:174
  45.3 0.3 prepare.1
  45.6 0.0 collective-permute-done.2.refs_2_
  45.6 0.0 collective-permute-done.1.refs_1_
  45.7 0.0 copy-done
  45.7 1.0 %add_part.1.total_ref = f32[500,1024]{1,0:T(8,128)S(1)} custom-call(bf16[500,576]{1,0:T(8,128)(2,1)S(1)} %get-tuple-element.8.left_ref, f32[500,1024]{1,0:T(8,128)S(1)} %bitcast.4, f32[64,1024]{1,0:T(8,128)S(1)} %stacked.1.refs_0_, f32[64,1024]{1,0:T(8,128)S(1)} %collective-permute-done.1.refs_1_, f32[64,1024]{1,0:T(8,128)S(1)} %collective-permute-done.2.refs_2_), custom_call_target="tpu_custom_call" | custom-call | flops 589824000 | bytes 4096000 | tf_op jit(solution)/shard_map/add_part/pallas_call | solution.py:115
  46.7 0.0 collective-permute-done.3.refs_0_
  46.7 1.6 %add_last.1 = f32[500,1024]{1,0:T(8,128)} custom-call(bf16[500,192]{1,0:T(8,128)(2,1)S(1)} %get-tuple-element.7.left_ref, f32[500,1024]{1,0:T(8,128)S(1)} %add_part.1.total_ref, f32[64,1024]{1,0:T(8,128)S(1)} %collective-permute-done.3.refs_0_), custom_call_target="tpu_custom_call" | custom-call | flops 196608000 | bytes 4096000 | tf_op jit(solution)/shard_map/add_last/pallas_call | solution.py:142
  (1 shorter events, 0.0 us)
Async XLA Ops:
  7.7 19.7 %collective-permute-start = (f32[32,1024]{1,0:T(8,128)S(1)}, f32[32,1024]{1,0:T(8,128)S(1)}, u32[]{:S(2)}, u32[]{:S(2)}) collective-permute-start(f32[32,1024]{1,0:T(8,128)S(1)} %all_gather.7.refs_0_), channel_id=1, source_target_pairs={{4,0},{13,1},{6,2},{15,3},{8,4},{1,5},{10,6},{3,7},{12,8},{5,9},{1... | collective-permute-start | bytes 393224 | tf_op jit(solution)/shard_map/ppermute | solution.py:165
  19.1 0.7 %copy-start.1 = (f32[8,500]{1,0:T(8,128)S(1)}, f32[8,500]{1,0:T(8,128)}, u32[]{:S(2)}) copy-start(f32[8,500]{1,0:T(8,128)} %block_ref.1) | copy-start | bytes 48004
  20.7 20.6 %all-to-all-start = ((f32[16,8,500]{2,1,0:T(8,128)}), f32[16,8,500]{2,1,0:T(8,128)S(1)}, u32[]{:S(2)}, u32[]{:S(2)}) async-start(f32[16,8,500]{2,1,0:T(8,128)} %copies.1), calls=%async_computation | async-start | bytes 524288 | tf_op jit(solution)/shard_map/all_to_all | solution.py:168
  27.4 18.2 %copy-start = (f32[1024,500]{0,1:T(8,128)S(1)}, f32[1024,500]{0,1:T(8,128)}, u32[]{:S(2)}) copy-start(f32[1024,500]{0,1:T(8,128)} %param.5) | copy-start | bytes 6144004
  27.5 18.2 %collective-permute-start.2 = (f32[64,1024]{1,0:T(8,128)S(1)}, f32[64,1024]{1,0:T(8,128)S(1)}, u32[]{:S(2)}, u32[]{:S(2)}) collective-permute-start(f32[64,1024]{1,0:T(8,128)S(1)} %stacked.1.refs_0_), channel_id=1, source_target_pairs={{2,0},{15,1},{4,2},{1,3},{6,4},{3,5},{8,6},{5,7},{10,8},{7,9},{12,... | collective-permute-start | bytes 786440 | tf_op jit(solution)/shard_map/ppermute | solution.py:165
  34.7 10.9 %collective-permute-start.1 = (f32[64,1024]{1,0:T(8,128)S(1)}, f32[64,1024]{1,0:T(8,128)S(1)}, u32[]{:S(2)}, u32[]{:S(2)}) collective-permute-start(f32[64,1024]{1,0:T(8,128)S(1)} %stacked.1.refs_0_), channel_id=1, source_target_pairs={{15,0},{0,1},{1,2},{2,3},{3,4},{4,5},{5,6},{6,7},{7,8},{8,9},{9,10... | collective-permute-start | bytes 786440 | tf_op jit(solution)/shard_map/ppermute | solution.py:165
  36.7 10.0 %collective-permute-start.3 = (f32[64,1024]{1,0:T(8,128)S(1)}, f32[64,1024]{1,0:T(8,128)S(1)}, u32[]{:S(2)}, u32[]{:S(2)}) collective-permute-start(f32[64,1024]{1,0:T(8,128)S(1)} %stacked.1.refs_0_), channel_id=1, source_target_pairs={{1,0},{2,1},{3,2},{4,3},{5,4},{6,5},{7,6},{8,7},{9,8},{10,9},{11,1... | collective-permute-start | bytes 786440 | tf_op jit(solution)/shard_map/ppermute | solution.py:165

commit v5 on v4

--- a/solution.py
+++ b/solution.py
@@ -9,9 +9,9 @@
 LONG = 10**11
 
 PAIR = 3
-HOP = (4, -4)
-HELD = ((0, -3), (3, 0), (4, -7), (7, -4))
-FROM = ((0, 0), (-1, -1), (2, -2), (1, 1))
+HOP = (-4, 4)
+HELD = ((-3, 0), (0, 3), (-7, 4), (-4, 7))
+FROM = ((0, 0), (-1, -1), (-2, 2), (1, 1))
 
 
 def halves(values):
@@ -31,26 +31,6 @@
 
 def cost(flops, moved):
     return pl.CostEstimate(flops=flops, bytes_accessed=moved, transcendentals=0)
-
-
-def copies(block, count):
-    def kernel(block_ref, out_ref, sems):
-        stores = [pltpu.make_async_copy(block_ref, out_ref.at[i], sems.at[i]) for i in range(count)]
-        for store in stores:
-            store.start()
-        for store in stores:
-            store.wait()
-
-    return pl.pallas_call(
-        kernel,
-        out_shape=jax.ShapeDtypeStruct((count,) + block.shape, block.dtype),
-        in_specs=[pl.BlockSpec(memory_space=pltpu.VMEM)],
-        out_specs=pl.BlockSpec(memory_space=pl.ANY),
-        scratch_shapes=[pltpu.SemaphoreType.DMA((count,))],
-        compiler_params=pltpu.CompilerParams(vmem_limit_bytes=8 << 20),
-        cost_estimate=cost(LONG, count * block.size * 4),
-        name="copies",
-    )(block)
 
 
 def stacked(blocks):
@@ -165,9 +145,10 @@
         return lax.ppermute(block, ("rows", "bands"), pairs)
 
     def local(psi_panels, rotation, accumulated):
-        spread = lax.all_to_all(copies(rotation, chips), "rows", 0, 0, axis_index_groups=same_core)
+        copies = jnp.broadcast_to(rotation[None], (chips,) + rotation.shape)
+        spread = lax.all_to_all(copies, "rows", 0, 0, axis_index_groups=same_core)
         spread = spread.reshape(-1, rotation.shape[1])
-        pairs = [[z, (z + PAIR) % levels] for z in range(0, levels, 2)]
+        pairs = [[z, (z + PAIR) % levels] for z in range(1, levels, 2)]
         couple = lax.all_gather(psi_panels.T, "bands", axis=0, tiled=True, axis_index_groups=pairs)
         own = stacked([couple, fetched(couple, HOP)])
         below, across, above = [fetched(own, offsets) for offsets in FROM[1:]]

time: 48.7 us -> 48.3 us (level)
  the two profiles are of different devices: /device:TPU:1 before, /device:TPU:2 now
where the time goes in v5:
time: 48.3 us; the launch traced here: 47.8 us
  starting transfers between devices  24.2 us (50%)
  blocking collectives  16.4 us (34%)
  Pallas kernels  2.89 us (6%)
  waiting for transfers between devices  2.81 us (6%)
  local copies, waits for them, and re-layouts  1.45 us (3%)
    ppermute x4, starting transfers between devices, fetched(): return lax.ppermute(block, ('rows', 'bands'), pairs)  16.7 us
    all_gather x1, blocking collectives, local(): lax.all_gather(psi_panels.T, 'bands', axis=0, tiled=True, axis_index_grou...  14.3 us
    all_to_all x1, starting transfers between devices, local(): spread = lax.all_to_all(copies, 'rows', 0, 0, axis_index_groups=same_core)  7.48 us
    ppermute x4, waiting for transfers between devices, fetched(): return lax.ppermute(block, ('rows', 'bands'), pairs)  2.81 us
    all_gather x1, blocking collectives, local(): lax.all_gather(spread, 'rows', axis=0, tiled=True, axis_index_groups=same...  2.18 us
    pallas_call x1, Pallas kernels, add_last(): pl.pallas_call(kernel, out_shape=jax.ShapeDtypeStruct(total.shape, jnp.fl...  1.56 us
    broadcast_in_dim x1, local copies, waits for them, and re-layouts, local(): copies = jnp.broadcast_to(rotation[None], (chips,) + rotation.shape)  1.45 us
    pallas_call x1, Pallas kernels, add_part(): pl.pallas_call(kernel, out_shape=jax.ShapeDtypeStruct(total.shape, jnp.fl...  0.99 us
  transfers between devices with their start and end apart: 5, of which 2 were waited for; matrix products, arithmetic and copies ran while one was open for 3% of the time, Pallas kernels for 3%

profile of v5, /device:TPU:2, one launch (start us, length us, event | category | flops | bytes accessed | tf_op | source)
XLA Modules:
  0.0 47.8 jit_solution(10749474611450208005)
XLA Ops:
  0.0 14.3 %all_gather.7.refs_0_ = f32[32,1024]{1,0:T(8,128)S(1)} all-gather(f32[16,1024]{1,0:T(8,128)} %bitcast.6), channel_id=1, replica_groups={{1,4},{3,6},{5,8},{7,10},{9,12},{11,14},{13,0},{15,2},{17,20},{19,22},{..., dimensions={0}, use_global_device_ids=true | all-gather | bytes 196608 | tf_op jit(solution)/shard_map/all_gather | solution.py:152
  14.3 3.1 %collective-permute-start = (f32[32,1024]{1,0:T(8,128)S(1)}, f32[32,1024]{1,0:T(8,128)S(1)}, u32[]{:S(2)}, u32[]{:S(2)}) collective-permute-start(f32[32,1024]{1,0:T(8,128)S(1)} %all_gather.7.refs_0_), channel_id=1, source_target_pairs={{12,0},{5,1},{14,2},{7,3},{0,4},{9,5},{2,6},{11,7},{4,8},{13,9},{6... | collective-permute-start | bytes 393224 | tf_op jit(solution)/shard_map/ppermute | solution.py:145
  17.3 1.4 %broadcast_in_dim.2 = f32[16,8,500]{2,1,0:T(8,128)} broadcast(f32[8,500]{1,0:T(8,128)} %param.4), dimensions={1,2} | broadcast | bytes 272000 | tf_op jit(solution)/shard_map/broadcast_in_dim | solution.py:148
  18.8 7.5 %all-to-all-start = ((f32[16,8,500]{2,1,0:T(8,128)}), f32[16,8,500]{2,1,0:T(8,128)S(1)}, u32[]{:S(2)}, u32[]{:S(2)}) async-start(f32[16,8,500]{2,1,0:T(8,128)} %broadcast_in_dim.2), calls=%async_computation | async-start | bytes 524288 | tf_op jit(solution)/shard_map/all_to_all | solution.py:149
  26.3 0.0 collective-permute-done.refs_1_
  26.3 0.0 copy-start
  26.3 5.6 %collective-permute-start.2 = (f32[64,1024]{1,0:T(8,128)S(1)}, f32[64,1024]{1,0:T(8,128)S(1)}, u32[]{:S(2)}, u32[]{:S(2)}) collective-permute-start(f32[64,1024]{1,0:T(8,128)S(1)} %stacked.1.refs_0_), channel_id=1, source_target_pairs={{14,0},{3,1},{0,2},{5,3},{2,4},{7,5},{4,6},{9,7},{6,8},{11,9},{8,1... | collective-permute-start | bytes 786440 | tf_op jit(solution)/shard_map/ppermute | solution.py:145
  31.9 6.1 %collective-permute-start.1 = (f32[64,1024]{1,0:T(8,128)S(1)}, f32[64,1024]{1,0:T(8,128)S(1)}, u32[]{:S(2)}, u32[]{:S(2)}) collective-permute-start(f32[64,1024]{1,0:T(8,128)S(1)} %stacked.1.refs_0_), channel_id=1, source_target_pairs={{15,0},{0,1},{1,2},{2,3},{3,4},{4,5},{5,6},{6,7},{7,8},{8,9},{9,10... | collective-permute-start | bytes 786440 | tf_op jit(solution)/shard_map/ppermute | solution.py:145
  38.0 1.9 %collective-permute-start.3 = (f32[64,1024]{1,0:T(8,128)S(1)}, f32[64,1024]{1,0:T(8,128)S(1)}, u32[]{:S(2)}, u32[]{:S(2)}) collective-permute-start(f32[64,1024]{1,0:T(8,128)S(1)} %stacked.1.refs_0_), channel_id=1, source_target_pairs={{1,0},{2,1},{3,2},{4,3},{5,4},{6,5},{7,6},{8,7},{9,8},{10,9},{11,1... | collective-permute-start | bytes 786440 | tf_op jit(solution)/shard_map/ppermute | solution.py:145
  39.9 0.0 all-to-all-done
  39.9 2.2 %all_gather.6.rotation_ref = f32[256,500]{1,0:T(8,128)S(1)} all-gather(f32[128,500]{1,0:T(8,128)S(1)} %bitcast.5), channel_id=1, replica_groups={{0,16},{32,48},{64,80},{96,112},{128,144},{160,176},{192,208},{224,240}..., dimensions={0}, use_global_device_ids=true | all-gather | bytes 768000 | tf_op jit(solution)/shard_map/all_gather | solution.py:155
  42.1 0.3 prepare.1
  42.5 0.0 collective-permute-done.2.refs_2_
  42.5 0.5 %collective-permute-done.1.refs_1_ = f32[64,1024]{1,0:T(8,128)S(1)} collective-permute-done((f32[64,1024]{1,0:T(8,128)S(1)}, f32[64,1024]{1,0:T(8,128)S(1)}, u32[]{:S(2)}, u32[]{:S(2)}) %collective-permute-start.1) | collective-permute-done | bytes 262176 | tf_op jit(solution)/shard_map/ppermute | solution.py:145
  43.0 0.0 copy-done
  43.0 1.0 %add_part.1.total_ref = f32[500,1024]{1,0:T(8,128)S(1)} custom-call(bf16[500,576]{1,0:T(8,128)(2,1)S(1)} %get-tuple-element.8.left_ref, f32[500,1024]{1,0:T(8,128)S(1)} %bitcast.4, f32[64,1024]{1,0:T(8,128)S(1)} %stacked.1.refs_0_, f32[64,1024]{1,0:T(8,128)S(1)} %collective-permute-done.1.refs_1_, f32[64,1024]{1,0:T(8,128)S(1)} %collective-permute-done.2.refs_2_), custom_call_target="tpu_custom_call" | custom-call | flops 589824000 | bytes 4096000 | tf_op jit(solution)/shard_map/add_part/pallas_call | solution.py:95
  44.0 2.3 %collective-permute-done.3.refs_0_ = f32[64,1024]{1,0:T(8,128)S(1)} collective-permute-done((f32[64,1024]{1,0:T(8,128)S(1)}, f32[64,1024]{1,0:T(8,128)S(1)}, u32[]{:S(2)}, u32[]{:S(2)}) %collective-permute-start.3) | collective-permute-done | bytes 262176 | tf_op jit(solution)/shard_map/ppermute | solution.py:145
  46.3 1.6 %add_last.1 = f32[500,1024]{1,0:T(8,128)} custom-call(bf16[500,192]{1,0:T(8,128)(2,1)S(1)} %get-tuple-element.7.left_ref, f32[500,1024]{1,0:T(8,128)S(1)} %add_part.1.total_ref, f32[64,1024]{1,0:T(8,128)S(1)} %collective-permute-done.3.refs_0_), custom_call_target="tpu_custom_call" | custom-call | flops 196608000 | bytes 4096000 | tf_op jit(solution)/shard_map/add_last/pallas_call | solution.py:122
  (1 shorter events, 0.0 us)
Async XLA Ops:
  14.3 12.0 %collective-permute-start = (f32[32,1024]{1,0:T(8,128)S(1)}, f32[32,1024]{1,0:T(8,128)S(1)}, u32[]{:S(2)}, u32[]{:S(2)}) collective-permute-start(f32[32,1024]{1,0:T(8,128)S(1)} %all_gather.7.refs_0_), channel_id=1, source_target_pairs={{12,0},{5,1},{14,2},{7,3},{0,4},{9,5},{2,6},{11,7},{4,8},{13,9},{6... | collective-permute-start | bytes 393224 | tf_op jit(solution)/shard_map/ppermute | solution.py:145
  18.8 21.1 %all-to-all-start = ((f32[16,8,500]{2,1,0:T(8,128)}), f32[16,8,500]{2,1,0:T(8,128)S(1)}, u32[]{:S(2)}, u32[]{:S(2)}) async-start(f32[16,8,500]{2,1,0:T(8,128)} %broadcast_in_dim.2), calls=%async_computation | async-start | bytes 524288 | tf_op jit(solution)/shard_map/all_to_all | solution.py:149
  26.3 16.7 %copy-start = (f32[1024,500]{0,1:T(8,128)S(1)}, f32[1024,500]{0,1:T(8,128)}, u32[]{:S(2)}) copy-start(f32[1024,500]{0,1:T(8,128)} %param.5) | copy-start | bytes 6144004
  26.3 16.1 %collective-permute-start.2 = (f32[64,1024]{1,0:T(8,128)S(1)}, f32[64,1024]{1,0:T(8,128)S(1)}, u32[]{:S(2)}, u32[]{:S(2)}) collective-permute-start(f32[64,1024]{1,0:T(8,128)S(1)} %stacked.1.refs_0_), channel_id=1, source_target_pairs={{14,0},{3,1},{0,2},{5,3},{2,4},{7,5},{4,6},{9,7},{6,8},{11,9},{8,1... | collective-permute-start | bytes 786440 | tf_op jit(solution)/shard_map/ppermute | solution.py:145
  31.9 11.1 %collective-permute-start.1 = (f32[64,1024]{1,0:T(8,128)S(1)}, f32[64,1024]{1,0:T(8,128)S(1)}, u32[]{:S(2)}, u32[]{:S(2)}) collective-permute-start(f32[64,1024]{1,0:T(8,128)S(1)} %stacked.1.refs_0_), channel_id=1, source_target_pairs={{15,0},{0,1},{1,2},{2,3},{3,4},{4,5},{5,6},{6,7},{7,8},{8,9},{9,10... | collective-permute-start | bytes 786440 | tf_op jit(solution)/shard_map/ppermute | solution.py:145
  38.0 8.3 %collective-permute-start.3 = (f32[64,1024]{1,0:T(8,128)S(1)}, f32[64,1024]{1,0:T(8,128)S(1)}, u32[]{:S(2)}, u32[]{:S(2)}) collective-permute-start(f32[64,1024]{1,0:T(8,128)S(1)} %stacked.1.refs_0_), channel_id=1, source_target_pairs={{1,0},{2,1},{3,2},{4,3},{5,4},{6,5},{7,6},{8,7},{9,8},{10,9},{11,1... | collective-permute-start | bytes 786440 | tf_op jit(solution)/shard_map/ppermute | solution.py:145

commit v6 on v5

--- a/solution.py
+++ b/solution.py
@@ -11,7 +11,7 @@
 PAIR = 3
 HOP = (-4, 4)
 HELD = ((-3, 0), (0, 3), (-7, 4), (-4, 7))
-FROM = ((0, 0), (-1, -1), (-2, 2), (1, 1))
+FROM = ((0, 0), (-1, 1), (-2, 2), (1, -1))
 
 
 def halves(values):
@@ -151,11 +151,11 @@
         pairs = [[z, (z + PAIR) % levels] for z in range(1, levels, 2)]
         couple = lax.all_gather(psi_panels.T, "bands", axis=0, tiled=True, axis_index_groups=pairs)
         own = stacked([couple, fetched(couple, HOP)])
-        below, across, above = [fetched(own, offsets) for offsets in FROM[1:]]
+        first, across, second = [fetched(own, offsets) for offsets in FROM[1:]]
         rot_whole = lax.all_gather(spread, "rows", axis=0, tiled=True, axis_index_groups=same_chip)
         early, late = prepare(rot_whole, levels, cores, (FROM[:3], FROM[3:]))
-        total = add_part(early, accumulated.T, (own, below, across))
-        return add_last(late, total, (above,)).T
+        total = add_part(early, accumulated.T, (own, first, across))
+        return add_last(late, total, (second,)).T
 
     spec = P("rows", "bands")
     return jax.shard_map(local, mesh=mesh, in_specs=(spec, spec, spec), out_specs=spec, check_vma=False)

time: 48.3 us -> 48.3 us (level)
  waiting for transfers between devices: 2.81 us -> 1.68 us
  starting transfers between devices: 24.2 us -> 25.3 us
    ppermute x4, waiting for transfers between devices: 2.81 us -> 1.68 us  [fetched(): return lax.ppermute(block, ('rows', 'bands'), pairs)]
    ppermute x4, starting transfers between devices: 16.7 us -> 17.8 us  [fetched(): return lax.ppermute(block, ('rows', 'bands'), pairs)]
where the time goes in v6:
time: 48.3 us; the launch traced here: 47.8 us
  starting transfers between devices  25.3 us (52%)
  blocking collectives  16.4 us (34%)
  Pallas kernels  2.88 us (6%)
  waiting for transfers between devices  1.68 us (3%)
  local copies, waits for them, and re-layouts  1.45 us (3%)
    ppermute x4, starting transfers between devices, fetched(): return lax.ppermute(block, ('rows', 'bands'), pairs)  17.8 us
    all_gather x1, blocking collectives, local(): lax.all_gather(psi_panels.T, 'bands', axis=0, tiled=True, axis_index_grou...  14.3 us
    all_to_all x1, starting transfers between devices, local(): spread = lax.all_to_all(copies, 'rows', 0, 0, axis_index_groups=same_core)  7.48 us
    all_gather x1, blocking collectives, local(): lax.all_gather(spread, 'rows', axis=0, tiled=True, axis_index_groups=same...  2.18 us
    ppermute x4, waiting for transfers between devices, fetched(): return lax.ppermute(block, ('rows', 'bands'), pairs)  1.68 us
    pallas_call x1, Pallas kernels, add_last(): pl.pallas_call(kernel, out_shape=jax.ShapeDtypeStruct(total.shape, jnp.fl...  1.56 us
    broadcast_in_dim x1, local copies, waits for them, and re-layouts, local(): copies = jnp.broadcast_to(rotation[None], (chips,) + rotation.shape)  1.45 us
    pallas_call x1, Pallas kernels, add_part(): pl.pallas_call(kernel, out_shape=jax.ShapeDtypeStruct(total.shape, jnp.fl...  0.99 us
  transfers between devices with their start and end apart: 5, of which 2 were waited for; matrix products, arithmetic and copies ran while one was open for 3% of the time, Pallas kernels for 3%

profile of v6, /device:TPU:2, one launch (start us, length us, event | category | flops | bytes accessed | tf_op | source)
XLA Modules:
  0.0 47.8 jit_solution(11870201421450102442)
XLA Ops:
  0.0 14.3 %all_gather.7.refs_0_ = f32[32,1024]{1,0:T(8,128)S(1)} all-gather(f32[16,1024]{1,0:T(8,128)} %bitcast.6), channel_id=1, replica_groups={{1,4},{3,6},{5,8},{7,10},{9,12},{11,14},{13,0},{15,2},{17,20},{19,22},{..., dimensions={0}, use_global_device_ids=true | all-gather | bytes 196608 | tf_op jit(solution)/shard_map/all_gather | solution.py:152
  14.3 3.1 %collective-permute-start = (f32[32,1024]{1,0:T(8,128)S(1)}, f32[32,1024]{1,0:T(8,128)S(1)}, u32[]{:S(2)}, u32[]{:S(2)}) collective-permute-start(f32[32,1024]{1,0:T(8,128)S(1)} %all_gather.7.refs_0_), channel_id=1, source_target_pairs={{12,0},{5,1},{14,2},{7,3},{0,4},{9,5},{2,6},{11,7},{4,8},{13,9},{6... | collective-permute-start | bytes 393224 | tf_op jit(solution)/shard_map/ppermute | solution.py:145
  17.3 1.4 %broadcast_in_dim.2 = f32[16,8,500]{2,1,0:T(8,128)} broadcast(f32[8,500]{1,0:T(8,128)} %param.4), dimensions={1,2} | broadcast | bytes 272000 | tf_op jit(solution)/shard_map/broadcast_in_dim | solution.py:148
  18.8 7.5 %all-to-all-start = ((f32[16,8,500]{2,1,0:T(8,128)}), f32[16,8,500]{2,1,0:T(8,128)S(1)}, u32[]{:S(2)}, u32[]{:S(2)}) async-start(f32[16,8,500]{2,1,0:T(8,128)} %broadcast_in_dim.2), calls=%async_computation | async-start | bytes 524288 | tf_op jit(solution)/shard_map/all_to_all | solution.py:149
  26.3 0.0 collective-permute-done.refs_1_
  26.3 0.0 copy-start
  26.3 5.6 %collective-permute-start.2 = (f32[64,1024]{1,0:T(8,128)S(1)}, f32[64,1024]{1,0:T(8,128)S(1)}, u32[]{:S(2)}, u32[]{:S(2)}) collective-permute-start(f32[64,1024]{1,0:T(8,128)S(1)} %stacked.1.refs_0_), channel_id=1, source_target_pairs={{14,0},{3,1},{0,2},{5,3},{2,4},{7,5},{4,6},{9,7},{6,8},{11,9},{8,1... | collective-permute-start | bytes 786440 | tf_op jit(solution)/shard_map/ppermute | solution.py:145
  31.9 6.1 %collective-permute-start.1 = (f32[64,1024]{1,0:T(8,128)S(1)}, f32[64,1024]{1,0:T(8,128)S(1)}, u32[]{:S(2)}, u32[]{:S(2)}) collective-permute-start(f32[64,1024]{1,0:T(8,128)S(1)} %stacked.1.refs_0_), channel_id=1, source_target_pairs={{15,0},{2,1},{1,2},{4,3},{3,4},{6,5},{5,6},{8,7},{7,8},{10,9},{9,1... | collective-permute-start | bytes 786440 | tf_op jit(solution)/shard_map/ppermute | solution.py:145
  38.0 3.1 %collective-permute-start.3 = (f32[64,1024]{1,0:T(8,128)S(1)}, f32[64,1024]{1,0:T(8,128)S(1)}, u32[]{:S(2)}, u32[]{:S(2)}) collective-permute-start(f32[64,1024]{1,0:T(8,128)S(1)} %stacked.1.refs_0_), channel_id=1, source_target_pairs={{1,0},{0,1},{3,2},{2,3},{5,4},{4,5},{7,6},{6,7},{9,8},{8,9},{11,10... | collective-permute-start | bytes 786440 | tf_op jit(solution)/shard_map/ppermute | solution.py:145
  41.1 0.0 all-to-all-done
  41.1 2.2 %all_gather.6.rotation_ref = f32[256,500]{1,0:T(8,128)S(1)} all-gather(f32[128,500]{1,0:T(8,128)S(1)} %bitcast.5), channel_id=1, replica_groups={{0,16},{32,48},{64,80},{96,112},{128,144},{160,176},{192,208},{224,240}..., dimensions={0}, use_global_device_ids=true | all-gather | bytes 768000 | tf_op jit(solution)/shard_map/all_gather | solution.py:155
  43.2 0.3 prepare.1
  43.6 0.0 collective-permute-done.2.refs_2_
  43.6 0.7 %collective-permute-done.1.refs_1_ = f32[64,1024]{1,0:T(8,128)S(1)} collective-permute-done((f32[64,1024]{1,0:T(8,128)S(1)}, f32[64,1024]{1,0:T(8,128)S(1)}, u32[]{:S(2)}, u32[]{:S(2)}) %collective-permute-start.1) | collective-permute-done | bytes 262176 | tf_op jit(solution)/shard_map/ppermute | solution.py:145
  44.2 0.0 copy-done
  44.2 1.0 %add_part.1.total_ref = f32[500,1024]{1,0:T(8,128)S(1)} custom-call(bf16[500,576]{1,0:T(8,128)(2,1)S(1)} %get-tuple-element.8.left_ref, f32[500,1024]{1,0:T(8,128)S(1)} %bitcast.4, f32[64,1024]{1,0:T(8,128)S(1)} %stacked.1.refs_0_, f32[64,1024]{1,0:T(8,128)S(1)} %collective-permute-done.1.refs_1_, f32[64,1024]{1,0:T(8,128)S(1)} %collective-permute-done.2.refs_2_), custom_call_target="tpu_custom_call" | custom-call | flops 589824000 | bytes 4096000 | tf_op jit(solution)/shard_map/add_part/pallas_call | solution.py:95
  45.2 1.0 %collective-permute-done.3.refs_0_ = f32[64,1024]{1,0:T(8,128)S(1)} collective-permute-done((f32[64,1024]{1,0:T(8,128)S(1)}, f32[64,1024]{1,0:T(8,128)S(1)}, u32[]{:S(2)}, u32[]{:S(2)}) %collective-permute-start.3) | collective-permute-done | bytes 262176 | tf_op jit(solution)/shard_map/ppermute | solution.py:145
  46.3 1.6 %add_last.1 = f32[500,1024]{1,0:T(8,128)} custom-call(bf16[500,192]{1,0:T(8,128)(2,1)S(1)} %get-tuple-element.7.left_ref, f32[500,1024]{1,0:T(8,128)S(1)} %add_part.1.total_ref, f32[64,1024]{1,0:T(8,128)S(1)} %collective-permute-done.3.refs_0_), custom_call_target="tpu_custom_call" | custom-call | flops 196608000 | bytes 4096000 | tf_op jit(solution)/shard_map/add_last/pallas_call | solution.py:122
  (1 shorter events, 0.0 us)
Async XLA Ops:
  14.3 12.0 %collective-permute-start = (f32[32,1024]{1,0:T(8,128)S(1)}, f32[32,1024]{1,0:T(8,128)S(1)}, u32[]{:S(2)}, u32[]{:S(2)}) collective-permute-start(f32[32,1024]{1,0:T(8,128)S(1)} %all_gather.7.refs_0_), channel_id=1, source_target_pairs={{12,0},{5,1},{14,2},{7,3},{0,4},{9,5},{2,6},{11,7},{4,8},{13,9},{6... | collective-permute-start | bytes 393224 | tf_op jit(solution)/shard_map/ppermute | solution.py:145
  18.8 22.3 %all-to-all-start = ((f32[16,8,500]{2,1,0:T(8,128)}), f32[16,8,500]{2,1,0:T(8,128)S(1)}, u32[]{:S(2)}, u32[]{:S(2)}) async-start(f32[16,8,500]{2,1,0:T(8,128)} %broadcast_in_dim.2), calls=%async_computation | async-start | bytes 524288 | tf_op jit(solution)/shard_map/all_to_all | solution.py:149
  26.3 18.0 %copy-start = (f32[1024,500]{0,1:T(8,128)S(1)}, f32[1024,500]{0,1:T(8,128)}, u32[]{:S(2)}) copy-start(f32[1024,500]{0,1:T(8,128)} %param.5) | copy-start | bytes 6144004
  26.3 17.2 %collective-permute-start.2 = (f32[64,1024]{1,0:T(8,128)S(1)}, f32[64,1024]{1,0:T(8,128)S(1)}, u32[]{:S(2)}, u32[]{:S(2)}) collective-permute-start(f32[64,1024]{1,0:T(8,128)S(1)} %stacked.1.refs_0_), channel_id=1, source_target_pairs={{14,0},{3,1},{0,2},{5,3},{2,4},{7,5},{4,6},{9,7},{6,8},{11,9},{8,1... | collective-permute-start | bytes 786440 | tf_op jit(solution)/shard_map/ppermute | solution.py:145
  31.9 12.3 %collective-permute-start.1 = (f32[64,1024]{1,0:T(8,128)S(1)}, f32[64,1024]{1,0:T(8,128)S(1)}, u32[]{:S(2)}, u32[]{:S(2)}) collective-permute-start(f32[64,1024]{1,0:T(8,128)S(1)} %stacked.1.refs_0_), channel_id=1, source_target_pairs={{15,0},{2,1},{1,2},{4,3},{3,4},{6,5},{5,6},{8,7},{7,8},{10,9},{9,1... | collective-permute-start | bytes 786440 | tf_op jit(solution)/shard_map/ppermute | solution.py:145
  38.0 8.3 %collective-permute-start.3 = (f32[64,1024]{1,0:T(8,128)S(1)}, f32[64,1024]{1,0:T(8,128)S(1)}, u32[]{:S(2)}, u32[]{:S(2)}) collective-permute-start(f32[64,1024]{1,0:T(8,128)S(1)} %stacked.1.refs_0_), channel_id=1, source_target_pairs={{1,0},{0,1},{3,2},{2,3},{5,4},{4,5},{7,6},{6,7},{9,8},{8,9},{11,10... | collective-permute-start | bytes 786440 | tf_op jit(solution)/shard_map/ppermute | solution.py:145

commit v7 on v5

--- a/solution.py
+++ b/solution.py
@@ -6,7 +6,7 @@
 from jax.sharding import PartitionSpec as P
 
 TILE = 128
-LONG = 10**11
+LONG = 3 * 10**9
 
 PAIR = 3
 HOP = (-4, 4)

time: 48.3 us -> 48.3 us (level)
  no operation moved by 1% of the time
where the time goes in v7:
time: 48.3 us; the launch traced here: 47.8 us
  starting transfers between devices  24.2 us (50%)
  blocking collectives  16.4 us (34%)
  Pallas kernels  2.89 us (6%)
  waiting for transfers between devices  2.81 us (6%)
  local copies, waits for them, and re-layouts  1.45 us (3%)
    ppermute x4, starting transfers between devices, fetched(): return lax.ppermute(block, ('rows', 'bands'), pairs)  16.7 us
    all_gather x1, blocking collectives, local(): lax.all_gather(psi_panels.T, 'bands', axis=0, tiled=True, axis_index_grou...  14.3 us
    all_to_all x1, starting transfers between devices, local(): spread = lax.all_to_all(copies, 'rows', 0, 0, axis_index_groups=same_core)  7.48 us
    ppermute x4, waiting for transfers between devices, fetched(): return lax.ppermute(block, ('rows', 'bands'), pairs)  2.81 us
    all_gather x1, blocking collectives, local(): lax.all_gather(spread, 'rows', axis=0, tiled=True, axis_index_groups=same...  2.18 us
    pallas_call x1, Pallas kernels, add_last(): pl.pallas_call(kernel, out_shape=jax.ShapeDtypeStruct(total.shape, jnp.fl...  1.56 us
    broadcast_in_dim x1, local copies, waits for them, and re-layouts, local(): copies = jnp.broadcast_to(rotation[None], (chips,) + rotation.shape)  1.45 us
    pallas_call x1, Pallas kernels, add_part(): pl.pallas_call(kernel, out_shape=jax.ShapeDtypeStruct(total.shape, jnp.fl...  0.99 us
  transfers between devices with their start and end apart: 5, of which 2 were waited for; matrix products, arithmetic and copies ran while one was open for 3% of the time, Pallas kernels for 3%

profile of v7, /device:TPU:2, one launch (start us, length us, event | category | flops | bytes accessed | tf_op | source)
XLA Modules:
  0.0 47.8 jit_solution(10749474611450208005)
XLA Ops:
  0.0 14.3 %all_gather.7.refs_0_ = f32[32,1024]{1,0:T(8,128)S(1)} all-gather(f32[16,1024]{1,0:T(8,128)} %bitcast.6), channel_id=1, replica_groups={{1,4},{3,6},{5,8},{7,10},{9,12},{11,14},{13,0},{15,2},{17,20},{19,22},{..., dimensions={0}, use_global_device_ids=true | all-gather | bytes 196608 | tf_op jit(solution)/shard_map/all_gather | solution.py:152
  14.3 3.1 %collective-permute-start = (f32[32,1024]{1,0:T(8,128)S(1)}, f32[32,1024]{1,0:T(8,128)S(1)}, u32[]{:S(2)}, u32[]{:S(2)}) collective-permute-start(f32[32,1024]{1,0:T(8,128)S(1)} %all_gather.7.refs_0_), channel_id=1, source_target_pairs={{12,0},{5,1},{14,2},{7,3},{0,4},{9,5},{2,6},{11,7},{4,8},{13,9},{6... | collective-permute-start | bytes 393224 | tf_op jit(solution)/shard_map/ppermute | solution.py:145
  17.3 1.4 %broadcast_in_dim.2 = f32[16,8,500]{2,1,0:T(8,128)} broadcast(f32[8,500]{1,0:T(8,128)} %param.4), dimensions={1,2} | broadcast | bytes 272000 | tf_op jit(solution)/shard_map/broadcast_in_dim | solution.py:148
  18.8 7.5 %all-to-all-start = ((f32[16,8,500]{2,1,0:T(8,128)}), f32[16,8,500]{2,1,0:T(8,128)S(1)}, u32[]{:S(2)}, u32[]{:S(2)}) async-start(f32[16,8,500]{2,1,0:T(8,128)} %broadcast_in_dim.2), calls=%async_computation | async-start | bytes 524288 | tf_op jit(solution)/shard_map/all_to_all | solution.py:149
  26.3 0.0 collective-permute-done.refs_1_
  26.3 0.0 copy-start
  26.3 5.6 %collective-permute-start.2 = (f32[64,1024]{1,0:T(8,128)S(1)}, f32[64,1024]{1,0:T(8,128)S(1)}, u32[]{:S(2)}, u32[]{:S(2)}) collective-permute-start(f32[64,1024]{1,0:T(8,128)S(1)} %stacked.1.refs_0_), channel_id=1, source_target_pairs={{14,0},{3,1},{0,2},{5,3},{2,4},{7,5},{4,6},{9,7},{6,8},{11,9},{8,1... | collective-permute-start | bytes 786440 | tf_op jit(solution)/shard_map/ppermute | solution.py:145
  31.9 6.1 %collective-permute-start.1 = (f32[64,1024]{1,0:T(8,128)S(1)}, f32[64,1024]{1,0:T(8,128)S(1)}, u32[]{:S(2)}, u32[]{:S(2)}) collective-permute-start(f32[64,1024]{1,0:T(8,128)S(1)} %stacked.1.refs_0_), channel_id=1, source_target_pairs={{15,0},{0,1},{1,2},{2,3},{3,4},{4,5},{5,6},{6,7},{7,8},{8,9},{9,10... | collective-permute-start | bytes 786440 | tf_op jit(solution)/shard_map/ppermute | solution.py:145
  38.0 1.9 %collective-permute-start.3 = (f32[64,1024]{1,0:T(8,128)S(1)}, f32[64,1024]{1,0:T(8,128)S(1)}, u32[]{:S(2)}, u32[]{:S(2)}) collective-permute-start(f32[64,1024]{1,0:T(8,128)S(1)} %stacked.1.refs_0_), channel_id=1, source_target_pairs={{1,0},{2,1},{3,2},{4,3},{5,4},{6,5},{7,6},{8,7},{9,8},{10,9},{11,1... | collective-permute-start | bytes 786440 | tf_op jit(solution)/shard_map/ppermute | solution.py:145
  39.9 0.0 all-to-all-done
  39.9 2.2 %all_gather.6.rotation_ref = f32[256,500]{1,0:T(8,128)S(1)} all-gather(f32[128,500]{1,0:T(8,128)S(1)} %bitcast.5), channel_id=1, replica_groups={{0,16},{32,48},{64,80},{96,112},{128,144},{160,176},{192,208},{224,240}..., dimensions={0}, use_global_device_ids=true | all-gather | bytes 768000 | tf_op jit(solution)/shard_map/all_gather | solution.py:155
  42.1 0.3 prepare.1
  42.5 0.0 collective-permute-done.2.refs_2_
  42.5 0.5 %collective-permute-done.1.refs_1_ = f32[64,1024]{1,0:T(8,128)S(1)} collective-permute-done((f32[64,1024]{1,0:T(8,128)S(1)}, f32[64,1024]{1,0:T(8,128)S(1)}, u32[]{:S(2)}, u32[]{:S(2)}) %collective-permute-start.1) | collective-permute-done | bytes 262176 | tf_op jit(solution)/shard_map/ppermute | solution.py:145
  43.0 0.0 copy-done
  43.0 1.0 %add_part.1.total_ref = f32[500,1024]{1,0:T(8,128)S(1)} custom-call(bf16[500,576]{1,0:T(8,128)(2,1)S(1)} %get-tuple-element.8.left_ref, f32[500,1024]{1,0:T(8,128)S(1)} %bitcast.4, f32[64,1024]{1,0:T(8,128)S(1)} %stacked.1.refs_0_, f32[64,1024]{1,0:T(8,128)S(1)} %collective-permute-done.1.refs_1_, f32[64,1024]{1,0:T(8,128)S(1)} %collective-permute-done.2.refs_2_), custom_call_target="tpu_custom_call" | custom-call | flops 589824000 | bytes 4096000 | tf_op jit(solution)/shard_map/add_part/pallas_call | solution.py:95
  44.0 2.3 %collective-permute-done.3.refs_0_ = f32[64,1024]{1,0:T(8,128)S(1)} collective-permute-done((f32[64,1024]{1,0:T(8,128)S(1)}, f32[64,1024]{1,0:T(8,128)S(1)}, u32[]{:S(2)}, u32[]{:S(2)}) %collective-permute-start.3) | collective-permute-done | bytes 262176 | tf_op jit(solution)/shard_map/ppermute | solution.py:145
  46.3 1.6 %add_last.1 = f32[500,1024]{1,0:T(8,128)} custom-call(bf16[500,192]{1,0:T(8,128)(2,1)S(1)} %get-tuple-element.7.left_ref, f32[500,1024]{1,0:T(8,128)S(1)} %add_part.1.total_ref, f32[64,1024]{1,0:T(8,128)S(1)} %collective-permute-done.3.refs_0_), custom_call_target="tpu_custom_call" | custom-call | flops 196608000 | bytes 4096000 | tf_op jit(solution)/shard_map/add_last/pallas_call | solution.py:122
  (1 shorter events, 0.0 us)
Async XLA Ops:
  14.3 12.0 %collective-permute-start = (f32[32,1024]{1,0:T(8,128)S(1)}, f32[32,1024]{1,0:T(8,128)S(1)}, u32[]{:S(2)}, u32[]{:S(2)}) collective-permute-start(f32[32,1024]{1,0:T(8,128)S(1)} %all_gather.7.refs_0_), channel_id=1, source_target_pairs={{12,0},{5,1},{14,2},{7,3},{0,4},{9,5},{2,6},{11,7},{4,8},{13,9},{6... | collective-permute-start | bytes 393224 | tf_op jit(solution)/shard_map/ppermute | solution.py:145
  18.8 21.1 %all-to-all-start = ((f32[16,8,500]{2,1,0:T(8,128)}), f32[16,8,500]{2,1,0:T(8,128)S(1)}, u32[]{:S(2)}, u32[]{:S(2)}) async-start(f32[16,8,500]{2,1,0:T(8,128)} %broadcast_in_dim.2), calls=%async_computation | async-start | bytes 524288 | tf_op jit(solution)/shard_map/all_to_all | solution.py:149
  26.3 16.7 %copy-start = (f32[1024,500]{0,1:T(8,128)S(1)}, f32[1024,500]{0,1:T(8,128)}, u32[]{:S(2)}) copy-start(f32[1024,500]{0,1:T(8,128)} %param.5) | copy-start | bytes 6144004
  26.3 16.1 %collective-permute-start.2 = (f32[64,1024]{1,0:T(8,128)S(1)}, f32[64,1024]{1,0:T(8,128)S(1)}, u32[]{:S(2)}, u32[]{:S(2)}) collective-permute-start(f32[64,1024]{1,0:T(8,128)S(1)} %stacked.1.refs_0_), channel_id=1, source_target_pairs={{14,0},{3,1},{0,2},{5,3},{2,4},{7,5},{4,6},{9,7},{6,8},{11,9},{8,1... | collective-permute-start | bytes 786440 | tf_op jit(solution)/shard_map/ppermute | solution.py:145
  31.9 11.1 %collective-permute-start.1 = (f32[64,1024]{1,0:T(8,128)S(1)}, f32[64,1024]{1,0:T(8,128)S(1)}, u32[]{:S(2)}, u32[]{:S(2)}) collective-permute-start(f32[64,1024]{1,0:T(8,128)S(1)} %stacked.1.refs_0_), channel_id=1, source_target_pairs={{15,0},{0,1},{1,2},{2,3},{3,4},{4,5},{5,6},{6,7},{7,8},{8,9},{9,10... | collective-permute-start | bytes 786440 | tf_op jit(solution)/shard_map/ppermute | solution.py:145
  38.0 8.3 %collective-permute-start.3 = (f32[64,1024]{1,0:T(8,128)S(1)}, f32[64,1024]{1,0:T(8,128)S(1)}, u32[]{:S(2)}, u32[]{:S(2)}) collective-permute-start(f32[64,1024]{1,0:T(8,128)S(1)} %stacked.1.refs_0_), channel_id=1, source_target_pairs={{1,0},{2,1},{3,2},{4,3},{5,4},{6,5},{7,6},{8,7},{9,8},{10,9},{11,1... | collective-permute-start | bytes 786440 | tf_op jit(solution)/shard_map/ppermute | solution.py:145
